TPU v7x, 32 devices: a whole 2x2x4 slice. The times are simulated.
32 devices in a mesh: ctx: 8 (over z, x), fsdp: 4 (over y, core).
Axes of the slice: x: 2, y: 2, z: 4, core: 2. Of those that a mesh axis runs over, the one named last changes fastest.
Arguments:
- tokens: bfloat16 [4, 2048, 1280], P('fsdp', 'ctx'), may hold values from -6 to 6
- lengths: int32 [4, 4], P('fsdp'), may hold values from 1 to 1024, 1920 in all within a row
- position: int32 [4, 2048], P('fsdp'), may hold values from 0 to 2047, as said below
- qkv_weight: bfloat16 [1280, 3840], P('fsdp'), may hold values from -0.15625 to 0.15625
- out_weight: bfloat16 [1280, 1280], P('fsdp'), may hold values from -0.5 to 0.5
- up_weight: bfloat16 [1280, 1280], P('fsdp'), may hold values from -0.15625 to 0.15625
- down_weight: bfloat16 [1280, 1280], P('fsdp'), may hold values from -0.15625 to 0.15625
- attn_gain: bfloat16 [1280], P('fsdp'), may hold values from 0.099609375 to 1.8984375
- mlp_gain: bfloat16 [1280], P('fsdp'), may hold values from 0.099609375 to 1.8984375
- query_scale: bfloat16 [80], P('fsdp'), may hold values from -3 to 3
- cotangent: bfloat16 [4, 2048, 1280], P('fsdp', 'ctx'), may hold values from -6 to 6
Outputs:
- output: float32 [4, 2048, 1280], P('fsdp', 'ctx')
- input_grad: float32 [4, 2048, 1280], P('fsdp', 'ctx')
- grad_qkv: float32 [1280, 3840], P('fsdp')
- grad_out: float32 [1280, 1280], P('fsdp')
- grad_up: float32 [1280, 1280], P('fsdp')
- grad_down: float32 [1280, 1280], P('fsdp')
- grad_attn_gain: float32 [1280], P('fsdp')
- grad_mlp_gain: float32 [1280], P('fsdp')
- grad_query_scale: float32 [80], P('fsdp')
Inputs may be any that keep to these rules, and one draw needn't show every extreme that they name: Each pack's sequences fill positions from 0 in order; positions from the sum of the lengths to the end are padding. Each row of position is a permutation of the pack's positions, and every run of 256 given rows of one index of ctx holds exactly 256 // 8 positions of each residue modulo 8.
All inputs are finite; a program needn't handle non-finite values.
Results may differ from a plain program's by a relative error of at most 0.04.
Values may be sent and summed in bfloat16 or wider, within the bound.
A program may use at most 256 MiB of HBM per device.

v0:
```python
import math

import jax
import jax.numpy as jnp
from jax import lax
from jax.sharding import PartitionSpec as P

HEADS = 16


EPS = 1e-06
FLOOR = -1e30
LOG2E = 1.442695041


def doc_index(places, seq_ends):
    return jnp.sum((places[:, None] >= seq_ends[None, :]).astype(jnp.int32), axis=1)


def spread_position(gathered_index, tok_dev, cycle_size):
    return gathered_index % tok_dev * cycle_size + gathered_index // tok_dev


def pair_scores(left_rows, right_rows):
    return jnp.einsum(
        "qhd,khd->qhk",
        left_rows.reshape(left_rows.shape[0], HEADS, -1),
        right_rows.reshape(right_rows.shape[0], HEADS, -1),
        preferred_element_type=jnp.float32,
    )


def pair_mask(query_pos, query_doc, key_pos, key_doc):
    return ((query_doc[:, None] == key_doc[None, :]) & (key_pos[None, :] <= query_pos[:, None]))[
        :, None, :
    ]


def in_blocks(advance, carried, pieces):
    total_rows = pieces[0].shape[0]
    block_rows = math.gcd(total_rows, 1024)
    block_count = total_rows // block_rows
    split = tuple((p.reshape((block_count, block_rows) + p.shape[1:]) for p in pieces))

    def inner(running, entry):
        return (advance(running, entry[1], entry[0] * block_rows), None)

    result, unused = lax.scan(inner, carried, (jnp.arange(block_count, dtype=jnp.int32), split))
    return result


def pair_terms(
    query_part,
    grad_part,
    log_part,
    delta_part,
    query_pos,
    query_doc,
    key_part,
    value_part,
    key_pos,
    key_doc,
):
    visible = pair_mask(query_pos, query_doc, key_pos, key_doc)
    prob_float = jnp.where(
        visible, jnp.exp(pair_scores(query_part, key_part) - log_part[:, :, None]), 0.0
    )
    grad_probs = pair_scores(grad_part, value_part)
    score_grad = (prob_float * (grad_probs - delta_part[:, :, None])).astype(jnp.bfloat16)
    return (prob_float.astype(jnp.bfloat16), score_grad)


def body(
    tokens,
    lengths,
    position,
    qkv_weight,
    out_weight,
    up_weight,
    down_weight,
    attn_gain,
    mlp_gain,
    query_scale,
    cotangent,
):
    cycle_size = lax.axis_size("ctx")
    my_index = lax.axis_index("ctx")
    tok_dev = tokens.shape[1]
    share_rows = tok_dev // cycle_size
    seq_ends = jnp.cumsum(lengths[0])
    place_row = position[0]
    residue = (place_row % cycle_size).reshape(cycle_size, tok_dev)
    landing = place_row // cycle_size
    matches = (
        residue[:, :, None] == jnp.arange(cycle_size, dtype=jnp.int32)[None, None, :]
    ).astype(jnp.int32)
    ranked = jnp.sum(jnp.cumsum(matches, axis=1) * matches, axis=2) - 1
    buffer_slot = residue * share_rows + ranked
    my_slots = lax.dynamic_index_in_dim(buffer_slot, my_index, 0, keepdims=False)
    local_rows = jnp.arange(tok_dev, dtype=jnp.int32)
    outgoing = jnp.zeros((tok_dev,), jnp.int32).at[my_slots].set(local_rows)
    flat_slot = (jnp.arange(cycle_size, dtype=jnp.int32)[:, None] * tok_dev + buffer_slot).reshape(
        -1
    )
    landing_table = (
        jnp.zeros((cycle_size * tok_dev,), jnp.int32)
        .at[flat_slot]
        .set(landing)
        .reshape(cycle_size, cycle_size, share_rows)
    )
    arrived_slot = lax.dynamic_index_in_dim(landing_table, my_index, 1, keepdims=False).reshape(-1)
    arrived_order = jnp.zeros((tok_dev,), jnp.int32).at[arrived_slot].set(local_rows)
    moved_x, moved_dy = (
        lax.all_to_all(tokens[0][outgoing], "ctx", split_axis=0, concat_axis=0, tiled=True),
        lax.all_to_all(cotangent[0][outgoing], "ctx", split_axis=0, concat_axis=0, tiled=True),
    )
    dealt_x = moved_x[arrived_order]
    dealt_dy = moved_dy[arrived_order]
    query_pos = local_rows * cycle_size + my_index
    query_doc = doc_index(query_pos, seq_ends)
    full_qkv, full_out, full_up, full_down, attn_gain_full, mlp_gain_full, scale_full = (
        lax.all_gather(qkv_weight, "fsdp", axis=0, tiled=True),
        lax.all_gather(out_weight, "fsdp", axis=0, tiled=True),
        lax.all_gather(up_weight, "fsdp", axis=0, tiled=True),
        lax.all_gather(down_weight, "fsdp", axis=0, tiled=True),
        lax.all_gather(attn_gain, "fsdp", axis=0, tiled=True),
        lax.all_gather(mlp_gain, "fsdp", axis=0, tiled=True),
        lax.all_gather(query_scale, "fsdp", axis=0, tiled=True),
    )
    attn_gain_f = attn_gain_full.astype(jnp.float32)
    mlp_gain_f = mlp_gain_full.astype(jnp.float32)
    scale_float = scale_full.astype(jnp.float32)
    x_float = dealt_x.astype(jnp.float32)
    inv_attn = lax.rsqrt(jnp.mean(x_float * x_float, axis=1, keepdims=True) + EPS)
    normed_attn = (x_float * inv_attn * attn_gain_f).astype(jnp.bfloat16)
    projected = jnp.dot(normed_attn, full_qkv, preferred_element_type=jnp.float32)
    att_width = projected.shape[1] // 3
    head_dim = scale_full.shape[0]
    base_scale = LOG2E / math.sqrt(head_dim)
    multiplier = jnp.tile(base_scale * jax.nn.softplus(scale_float), att_width // head_dim)
    raw_query = projected[:, :att_width]
    queries = (raw_query * multiplier).astype(jnp.bfloat16)
    key_rows = projected[:, att_width : 2 * att_width].astype(jnp.bfloat16)
    value_rows = projected[:, 2 * att_width :].astype(jnp.bfloat16)

    def key_place(first_row, amount):
        gathered_index = first_row + jnp.arange(amount, dtype=jnp.int32)
        key_pos = spread_position(gathered_index, tok_dev, cycle_size)
        return (key_pos, doc_index(key_pos, seq_ends))

    def stat_block(carried, pieces, first_row):
        running_max, running_sum = carried
        key_pos, key_doc = key_place(first_row, pieces[0].shape[0])
        visible = pair_mask(query_pos, query_doc, key_pos, key_doc)
        logits = jnp.where(visible, pair_scores(queries, pieces[0]), FLOOR)
        new_max = jnp.maximum(running_max, jnp.max(logits, axis=2))
        added = jnp.sum(jnp.where(visible, jnp.exp(logits - new_max[:, :, None]), 0.0), axis=2)
        return (new_max, running_sum * jnp.exp(running_max - new_max) + added)

    def output_block(summed, pieces, first_row):
        key_pos, key_doc = key_place(first_row, pieces[0].shape[0])
        visible = pair_mask(query_pos, query_doc, key_pos, key_doc)
        prob_low = jnp.where(
            visible, jnp.exp(pair_scores(queries, pieces[0]) - log_total[:, :, None]), 0.0
        ).astype(jnp.bfloat16)
        values_part = pieces[1].reshape(pieces[1].shape[0], HEADS, -1)
        return summed + jnp.einsum(
            "qhk,khd->qhd", prob_low, values_part, preferred_element_type=jnp.float32
        ).reshape(summed.shape)

    def query_grad_block(summed, pieces, first_row):
        key_pos, key_doc = key_place(first_row, pieces[0].shape[0])
        unused_probs, score_grad = pair_terms(
            queries,
            attended_grad,
            log_total,
            row_delta,
            query_pos,
            query_doc,
            pieces[0],
            pieces[1],
            key_pos,
            key_doc,
        )
        keys_part = pieces[0].reshape(pieces[0].shape[0], HEADS, -1)
        return summed + jnp.einsum(
            "qhk,khd->qhd", score_grad, keys_part, preferred_element_type=jnp.float32
        ).reshape(summed.shape)

    def key_grad_block(carried, pieces, first_row):
        amount = pieces[0].shape[0]
        part_pos, part_doc = key_place(first_row, amount)
        part_log = lax.dynamic_slice_in_dim(all_log, first_row, amount, 0)
        part_delta = lax.dynamic_slice_in_dim(all_delta, first_row, amount, 0)
        prob_low, score_grad = pair_terms(
            pieces[0],
            pieces[1],
            part_log,
            part_delta,
            part_pos,
            part_doc,
            key_rows,
            value_rows,
            query_pos,
            query_doc,
        )
        grad_keys = carried[0] + jnp.einsum(
            "qhk,qhd->khd",
            score_grad,
            pieces[0].reshape(amount, HEADS, -1),
            preferred_element_type=jnp.float32,
        ).reshape(tok_dev, -1)
        grad_values = carried[1] + jnp.einsum(
            "qhk,qhd->khd",
            prob_low,
            pieces[1].reshape(amount, HEADS, -1),
            preferred_element_type=jnp.float32,
        ).reshape(tok_dev, -1)
        return (grad_keys, grad_values)

    zero_stats = (
        jnp.full((tok_dev, HEADS), FLOOR, jnp.float32),
        jnp.zeros((tok_dev, HEADS), jnp.float32),
    )
    zero_rows = jnp.zeros((tok_dev, att_width), jnp.float32)
    running_max, running_sum = in_blocks(
        stat_block, zero_stats, (lax.all_gather(key_rows, "ctx", axis=0, tiled=True),)
    )
    log_total = running_max + jnp.log(running_sum)
    attended = in_blocks(
        output_block,
        zero_rows,
        (
            lax.all_gather(key_rows, "ctx", axis=0, tiled=True),
            lax.all_gather(value_rows, "ctx", axis=0, tiled=True),
        ),
    )
    attended_low = attended.astype(jnp.bfloat16)
    resid = x_float + jnp.dot(attended_low, full_out, preferred_element_type=jnp.float32)
    inv_mlp = lax.rsqrt(jnp.mean(resid * resid, axis=1, keepdims=True) + EPS)
    normed_mlp = (resid * inv_mlp * mlp_gain_f).astype(jnp.bfloat16)
    up_proj = jnp.dot(normed_mlp, full_up, preferred_element_type=jnp.float32)
    act_low = jax.nn.silu(up_proj).astype(jnp.bfloat16)
    result = resid + jnp.dot(act_low, full_down, preferred_element_type=jnp.float32)
    cot_float = dealt_dy.astype(jnp.float32)
    grad_down = jnp.dot(act_low.T, dealt_dy, preferred_element_type=jnp.float32)
    act_grad = jnp.dot(dealt_dy, full_down.T, preferred_element_type=jnp.float32)
    sigma = jax.nn.sigmoid(up_proj)
    up_grad = (act_grad * sigma * (1.0 + up_proj * (1.0 - sigma))).astype(jnp.bfloat16)
    grad_up = jnp.dot(normed_mlp.T, up_grad, preferred_element_type=jnp.float32)
    norm_mlp_grad = jnp.dot(up_grad, full_up.T, preferred_element_type=jnp.float32)
    grad_mlp_gain = jnp.sum(norm_mlp_grad * resid * inv_mlp, axis=0)
    scaled_mlp = norm_mlp_grad * mlp_gain_f
    resid_grad = cot_float + inv_mlp * (
        scaled_mlp - resid * inv_mlp * inv_mlp * jnp.mean(scaled_mlp * resid, axis=1, keepdims=True)
    )
    branch_grad = resid_grad.astype(jnp.bfloat16)
    grad_out = jnp.dot(attended_low.T, branch_grad, preferred_element_type=jnp.float32)
    attended_grad = jnp.dot(branch_grad, full_out.T, preferred_element_type=jnp.float32).astype(
        jnp.bfloat16
    )
    row_delta = jnp.sum(
        (attended_grad.astype(jnp.float32) * attended).reshape(tok_dev, HEADS, -1), axis=2
    )
    query_grads = in_blocks(
        query_grad_block,
        zero_rows,
        (
            lax.all_gather(key_rows, "ctx", axis=0, tiled=True),
            lax.all_gather(value_rows, "ctx", axis=0, tiled=True),
        ),
    )
    all_log, all_delta = (
        lax.all_gather(log_total, "ctx", axis=0, tiled=True),
        lax.all_gather(row_delta, "ctx", axis=0, tiled=True),
    )
    key_grad_f, value_grad_f = in_blocks(
        key_grad_block,
        (zero_rows, zero_rows),
        (
            lax.all_gather(queries, "ctx", axis=0, tiled=True),
            lax.all_gather(attended_grad, "ctx", axis=0, tiled=True),
        ),
    )
    scale_terms = jnp.sum((query_grads * raw_query).reshape(tok_dev, -1, head_dim), axis=(0, 1))
    grad_scale = scale_terms * base_scale * jax.nn.sigmoid(scale_float)
    proj_grad = jnp.concatenate(
        [
            (query_grads * multiplier).astype(jnp.bfloat16),
            key_grad_f.astype(jnp.bfloat16),
            value_grad_f.astype(jnp.bfloat16),
        ],
        axis=1,
    )
    grad_qkv = jnp.dot(normed_attn.T, proj_grad, preferred_element_type=jnp.float32)
    norm_attn_grad = jnp.dot(proj_grad, full_qkv.T, preferred_element_type=jnp.float32)
    grad_attn_gain = jnp.sum(norm_attn_grad * x_float * inv_attn, axis=0)
    scaled_attn = norm_attn_grad * attn_gain_f
    input_grad = resid_grad + inv_attn * (
        scaled_attn
        - x_float * inv_attn * inv_attn * jnp.mean(scaled_attn * x_float, axis=1, keepdims=True)
    )
    owned = (
        lax.psum_scatter(grad_qkv, "fsdp", scatter_dimension=0, tiled=True),
        lax.psum_scatter(grad_out, "fsdp", scatter_dimension=0, tiled=True),
        lax.psum_scatter(grad_up, "fsdp", scatter_dimension=0, tiled=True),
        lax.psum_scatter(grad_down, "fsdp", scatter_dimension=0, tiled=True),
        lax.psum_scatter(grad_attn_gain, "fsdp", scatter_dimension=0, tiled=True),
        lax.psum_scatter(grad_mlp_gain, "fsdp", scatter_dimension=0, tiled=True),
        lax.psum_scatter(grad_scale, "fsdp", scatter_dimension=0, tiled=True),
    )
    summed_grads = lax.psum(
        (owned[0], owned[1], owned[2], owned[3], owned[4], owned[5], owned[6]), "ctx"
    )
    back_out, back_grad = (
        lax.all_to_all(result[arrived_slot], "ctx", split_axis=0, concat_axis=0, tiled=True),
        lax.all_to_all(input_grad[arrived_slot], "ctx", split_axis=0, concat_axis=0, tiled=True),
    )
    return (
        back_out[my_slots][None],
        back_grad[my_slots][None],
        summed_grads[0],
        summed_grads[1],
        summed_grads[2],
        summed_grads[3],
        summed_grads[4],
        summed_grads[5],
        summed_grads[6],
    )


def solution(mesh):
    placed = (
        P("fsdp", "ctx", None),
        P("fsdp", None),
        P("fsdp", None),
        P("fsdp", None),
        P("fsdp", None),
        P("fsdp", None),
        P("fsdp", None),
        P("fsdp"),
        P("fsdp"),
        P("fsdp"),
        P("fsdp", "ctx", None),
    )
    return jax.shard_map(
        body,
        mesh=mesh,
        in_specs=placed,
        out_specs=(
            P("fsdp", "ctx", None),
            P("fsdp", "ctx", None),
            P("fsdp", None),
            P("fsdp", None),
            P("fsdp", None),
            P("fsdp", None),
            P("fsdp"),
            P("fsdp"),
            P("fsdp"),
        ),
        check_vma=False,
    )
```

profile of v0, /device:TPU:0, one launch (start us, length us, event | category | flops | bytes accessed | tf_op | source)
XLA Modules:
  0.0 1267.3 jit_solution(104251892187073882)
XLA Ops:
  52.3 27.0 %all-gather.9.cloned.1.call-done = bf16[1280,3840]{1,0:T(8,128)(2,1)} async-done(((bf16[320,3840]{1,0:T(8,128)(2,1)}), bf16[1280,3840]{1,0:T(8,128)(2,1)}) %all-gather.9.cloned.1.call-update) | async-done | bytes 9830416 | tf_op jit(solution)/shard_map/all_gather | solution.py:122
  79.2 8.5 fusion.113
  99.6 34.6 %all-to-all-done.2 = bf16[8,32,1280]{2,1,0:T(8,128)(2,1)S(1)} async-done(((bf16[8,32,1280]{2,1,0:T(8,128)(2,1)}), bf16[8,32,1280]{2,1,0:T(8,128)(2,1)S(1)}, u32[]{:S(2)}, u32[]{:S(2)}) %all-to-all-start.2) | async-done | bytes 655392 | tf_op jit(solution)/shard_map/all_to_all | solution.py:115
  138.8 50.5 %all-gather.13.cloned.1.call-done = bf16[2048,1280]{1,0:T(8,128)(2,1)} async-done(((bf16[256,1280]{1,0:T(8,128)(2,1)}), bf16[2048,1280]{1,0:T(8,128)(2,1)}) %all-gather.13.cloned.1.call-update) | async-done | bytes 5242896 | tf_op jit(solution)/shard_map/all_gather | solution.py:234
  197.4 42.7 %while.56 = (s32[]{:T(128)}, f32[256,16]{0,1:T(8,128)S(1)}, f32[256,16]{0,1:T(8,128)S(1)}, s32[256]{0:T(256)S(1)}, s32[2]{0:T(128)S(1)}, /*index=5*/s32[4]{0:T(1...) while((s32[]{:T(128)}, f32[256,16]{0,1:T(8,128)S(1)}, ...), condition=%wide.region_13.14_spmd.clone, body=%wide.region_9.13_spmd.clone.sunk | while | flops 697095680 | bytes 43097264 | solution.py:48
  209.3 9.2 select_reduce_fusion.2
  222.2 8.7 fusion.176
  230.9 9.2 select_reduce_fusion.2
  240.1 36.0 %all-gather.11.cloned.1.call-done = bf16[2048,1280]{1,0:T(8,128)(2,1)} async-done(((bf16[256,1280]{1,0:T(8,128)(2,1)}), bf16[2048,1280]{1,0:T(8,128)(2,1)}) %all-gather.11.cloned.1.call-update) | async-done | bytes 5242896 | tf_op jit(solution)/shard_map/all_gather | solution.py:235
  285.2 30.5 %while.57 = (s32[]{:T(128)}, f32[256,1280]{0,1:T(8,128)S(1)}, bf16[2,1024,1280]{1,2,0:T(8,128)(2,1)}, s32[256]{0:T(256)S(1)}, s32[2]{0:T(128)}, /*index=5*/s32[4...) while((s32[]{:T(128)}, f32[256,1280]{0,1:T(8,128)S(1)}, ...), condition=%wide.region_16.17_spmd.clone, body=%wide.region_14.16_spmd.clone.sunk | while | flops 1356236288 | bytes 22191288 | solution.py:48
  320.4 15.3 %all-gather.17.cloned.1.call-done = bf16[1280,1280]{1,0:T(8,128)(2,1)} async-done(((bf16[320,1280]{1,0:T(8,128)(2,1)}), bf16[1280,1280]{1,0:T(8,128)(2,1)}) %all-gather.17.cloned.1.call-update) | async-done | bytes 3276816 | tf_op jit(solution)/shard_map/all_gather | solution.py:124
  339.8 26.6 %all-gather.19.cloned.1.call-done = bf16[1280,1280]{1,0:T(8,128)(2,1)} async-done(((bf16[320,1280]{1,0:T(8,128)(2,1)}), bf16[1280,1280]{1,0:T(8,128)(2,1)}) %all-gather.19.cloned.1.call-update) | async-done | bytes 3276816 | tf_op jit(solution)/shard_map/all_gather | solution.py:125
  400.3 62.3 %while.58 = (s32[]{:T(128)}, f32[256,1280]{0,1:T(8,128)}, bf16[2,1024,1280]{1,2,0:T(8,128)(2,1)}, s32[256]{0:T(256)S(1)}, s32[2]{0:T(128)S(1)}, /*index=5*/s32[4...) while((s32[]{:T(128)}, f32[256,1280]{0,1:T(8,128)}, ...), condition=%wide.region_22.23_spmd.clone, body=%wide.region_20.22_spmd.clone.sunk | while | flops 2035713536 | bytes 59038920 | solution.py:48
  406.6 8.3 fusion.188
  414.9 13.8 %fusion.190 = f32[16,80,256]{2,1,0:T(8,128)} fusion(bf16[1024,16,80]{0,2,1:T(8,128)(2,1)S(1)} %bitcast.262, f32[16,1024,256]{2,1,0:T(8,128)} %fusion.188, bf16[1024,16,80]{0,2,1:T(8,128)(2,1)} %bitcast.271, bf16[256,16,80]{0,2,1:T(8,128)(2,1)} %bitcast.288, f32[256,16]{0,1:T(8,128)} %get-tuple-element.1490, f32[256,16]{0,1:T(8,128)} %get-tuple-element.1487, ...), kind=kOutput, calls=%fused_computation.71.clone.1 | convolution fusion | flops 1363148800 | bytes 24281088 | tf_op jit(solution)/shard_map/while/body/eval_jaxpr/qhk,khd->qhd/dot_general | solution.py:186
  445.8 13.7 %fusion.190 = f32[16,80,256]{2,1,0:T(8,128)} fusion(bf16[1024,16,80]{0,2,1:T(8,128)(2,1)S(1)} %bitcast.262, f32[16,1024,256]{2,1,0:T(8,128)} %fusion.188, bf16[1024,16,80]{0,2,1:T(8,128)(2,1)} %bitcast.271, bf16[256,16,80]{0,2,1:T(8,128)(2,1)} %bitcast.288, f32[256,16]{0,1:T(8,128)} %get-tuple-element.1490, f32[256,16]{0,1:T(8,128)} %get-tuple-element.1487, ...), kind=kOutput, calls=%fused_computation.71.clone.1 | convolution fusion | flops 1363148800 | bytes 24281088 | tf_op jit(solution)/shard_map/while/body/eval_jaxpr/qhk,khd->qhd/dot_general | solution.py:186
  464.4 33.2 %all_gather.54 = f32[2048,16]{0,1:T(8,128)} all-gather(f32[256,16]{0,1:T(8,128)S(1)} %copy-done.39), channel_id=1, replica_groups=mesh['ctx'=8,'fsdp'=4] {'ctx'}, dimensions={0}, use_global_device_ids=true | all-gather | bytes 147456 | tf_op jit(solution)/shard_map/all_gather | solution.py:275
  497.6 33.9 %all_gather.52 = f32[2048,16]{0,1:T(8,128)} all-gather(f32[256,16]{0,1:T(8,128)S(1)} %copy-done.40), channel_id=1, replica_groups=mesh['ctx'=8,'fsdp'=4] {'ctx'}, dimensions={0}, use_global_device_ids=true | all-gather | bytes 147456 | tf_op jit(solution)/shard_map/all_gather | solution.py:274
  534.5 10.3 all-gather.23.cloned.1.call-done
  544.9 108.7 %while.59 = (s32[]{:T(128)}, f32[256,1280]{0,1:T(8,128)}, f32[256,1280]{0,1:T(8,128)}, bf16[2,1024,1280]{2,1,0:T(8,128)(2,1)}, s32[2]{0:T(128)S(1)}, /*index=5*/...) while((s32[]{:T(128)}, f32[256,1280]{0,1:T(8,128)}, ...), condition=%wide.region_25.26_spmd.clone, body=%wide.region_23.25_spmd.clone.sunk | while | flops 2720040448 | bytes 115826040 | solution.py:48
  572.8 11.5 fusion.201
  584.2 9.4 fusion.200
  608.8 10.7 fusion.198
  627.5 12.6 fusion.201
  640.0 9.4 fusion.200
  656.4 9.4 fusion.75
  668.6 62.7 %reduce-scatter.11.cloned.1.call-done = f32[320,1280]{1,0:T(8,128)} async-done(((f32[1280,1280]{1,0:T(8,128)}), f32[320,1280]{1,0:T(8,128)}) %reduce-scatter.11.cloned.1.call-update) | async-done | bytes 1638416 | tf_op jit(solution)/shard_map/reduce_scatter | solution.py:307
  731.2 147.3 %reduce-scatter.5.cloned.1.call-done = f32[320,3840]{1,0:T(8,128)} async-done(((f32[1280,3840]{1,0:T(8,128)}), f32[320,3840]{1,0:T(8,128)}) %reduce-scatter.5.cloned.1.call-update) | async-done | bytes 4915216 | tf_op jit(solution)/shard_map/reduce_scatter | solution.py:304
  900.9 56.6 %all-to-all-done.1 = f32[8,32,1280]{2,1,0:T(8,128)S(1)} async-done(((f32[8,32,1280]{2,1,0:T(8,128)}), f32[8,32,1280]{2,1,0:T(8,128)S(1)}, u32[]{:S(2)}, u32[]{:S(2)}) %all-to-all-start.1) | async-done | bytes 1310752 | tf_op jit(solution)/shard_map/all_to_all | solution.py:316
  964.9 11.0 all-reduce.8
  976.2 44.3 %all-reduce.6 = (f32[320]{0:T(512)}, f32[320]{0:T(512)}, f32[20]{0:T(128)}) all-reduce(f32[320]{0:T(512)S(1)} %dynamic-slice.4, f32[320]{0:T(512)S(1)} %dynamic-slice.6, f32[20]{0:T(128)S(1)} %dynamic-slice.8), channel_id=1, replica_groups=mesh['ctx'=8,'fsdp'=4] {'ctx'}, use_global_device_ids=true, to_apply=%region_37.38 | all-reduce | flops 660 | bytes 5280 | tf_op jit(solution)/shard_map/psum | solution.py:312
  1024.1 225.9 %all-reduce.12.cloned.1.call-done = (f32[320,3840]{1,0:T(8,128)}, f32[320,1280]{1,0:T(8,128)}, f32[320,1280]{1,0:T(8,128)}, f32[320,1280]{1,0:T(8,128)}) async-done(((f32[320,3840]{1,0:T(8,128)}, f32[320,1280]{1,0:T(8,128)}, f32[320,1280]{1,0:T(8,128)}, f32[320,1280]{1,0:T(8,128)}), (f32[320,3840]{1,0:T(8,128)}, f32[320,1280]{1,0:T(8,128)}, f32[320,1280]{1,0:T(8,128)}, ...) | async-done | bytes 9830416 | tf_op jit(solution)/shard_map/psum | solution.py:312
  (343 shorter events, 294.0 us)
Async XLA Ops:
  7.2 16.9 %copy-start = (bf16[1,256,1280]{2,1,0:T(8,128)(2,1)S(1)}, bf16[1,256,1280]{2,1,0:T(8,128)(2,1)}, u32[]{:S(2)}) copy-start(bf16[1,256,1280]{2,1,0:T(8,128)(2,1)} %param.19) | copy-start | bytes 1966084
  7.2 72.0 %all-gather.9.cloned.1.call-start = ((), (), s32[]{:S(2)}) async-start(), calls=%async_computation.8 | async-start | bytes 12288000 | tf_op jit(solution)/shard_map/all_gather | solution.py:122
  22.6 21.2 %copy-start.47 = (s32[256,1]{0,1:T(1,128)}, s32[256,1]{0,1:T(1,128)S(1)}, u32[]{:S(2)}) copy-start(s32[256,1]{0,1:T(1,128)S(1)} %get-tuple-element.1038) | copy-start | bytes 3076
  24.1 11.9 copy-start.52
  26.2 24.6 %all-to-all-start = ((bf16[8,32,1280]{2,1,0:T(8,128)(2,1)}), bf16[8,32,1280]{2,1,0:T(8,128)(2,1)S(1)}, u32[]{:S(2)}, u32[]{:S(2)}) async-start(bf16[8,32,1280]{2,1,0:T(8,128)(2,1)} %bitcast.7), calls=%async_computation | async-start | bytes 1310720 | tf_op jit(solution)/shard_map/all_to_all | solution.py:114
  33.5 155.9 %all-gather.13.cloned.1.call-start = ((), (), s32[]{:S(2)}) async-start(), calls=%async_computation.10 | async-start | bytes 5898240 | tf_op jit(solution)/shard_map/all_gather | solution.py:234
  43.7 55.4 %copy-start.54 = (bf16[80]{0:T(256)(128)(2,1)}, bf16[80]{0:T(256)(128)(2,1)S(1)}, u32[]{:S(2)}) copy-start(bf16[80]{0:T(256)(128)(2,1)S(1)} %get-tuple-element.1012) | copy-start | bytes 484
  43.8 35.5 %copy-start.34 = (f32[1280]{0:T(1024)}, f32[1280]{0:T(1024)S(1)}, u32[]{:S(2)}) copy-start(f32[1280]{0:T(1024)S(1)} %convert_element_type.111) | copy-start | bytes 15364
  52.0 35.7 %copy-start.14 = (bf16[256,1280]{1,0:T(8,128)(2,1)}, bf16[256,1280]{1,0:T(8,128)(2,1)S(1)}, u32[]{:S(2)}) copy-start(bf16[256,1280]{1,0:T(8,128)(2,1)S(1)} %gather_fusion.1) | copy-start | bytes 1966084
  52.3 35.5 %copy-start.41 = (f32[256]{0:T(256)}, f32[256]{0:T(256)S(1)}, u32[]{:S(2)}) copy-start(f32[256]{0:T(256)S(1)} %add_rsqrt_fusion.1) | copy-start | bytes 3076
  89.0 187.1 %all-gather.11.cloned.1.call-start = ((), (), s32[]{:S(2)}) async-start(), calls=%async_computation.9 | async-start | bytes 5898240 | tf_op jit(solution)/shard_map/all_gather | solution.py:235
  89.7 227.5 %all-gather.15.cloned.1.call-start = ((), (), s32[]{:S(2)}) async-start(), calls=%async_computation.11 | async-start | bytes 4096000 | tf_op jit(solution)/shard_map/all_gather | solution.py:123
  90.3 245.4 %all-gather.17.cloned.1.call-start = ((), (), s32[]{:S(2)}) async-start(), calls=%async_computation.12 | async-start | bytes 4096000 | tf_op jit(solution)/shard_map/all_gather | solution.py:124
  90.9 275.5 %all-gather.19.cloned.1.call-start = ((), (), s32[]{:S(2)}) async-start(), calls=%async_computation.13 | async-start | bytes 4096000 | tf_op jit(solution)/shard_map/all_gather | solution.py:125
  93.6 40.6 %all-to-all-start.2 = ((bf16[8,32,1280]{2,1,0:T(8,128)(2,1)}), bf16[8,32,1280]{2,1,0:T(8,128)(2,1)S(1)}, u32[]{:S(2)}, u32[]{:S(2)}) async-start(bf16[8,32,1280]{2,1,0:T(8,128)(2,1)} %bitcast.23), calls=%async_computation.2 | async-start | bytes 1310720 | tf_op jit(solution)/shard_map/all_to_all | solution.py:115
  99.1 435.5 %all-gather.21.cloned.1.call-start = ((), (), s32[]{:S(2)}) async-start(), calls=%async_computation.14 | async-start | bytes 5898240 | tf_op jit(solution)/shard_map/all_gather | solution.py:281
  99.3 37.0 %copy-start.37 = (f32[1280]{0:T(1024)}, f32[1280]{0:T(1024)S(1)}, u32[]{:S(2)}) copy-start(f32[1280]{0:T(1024)S(1)} %mul.334) | copy-start | bytes 15364
  138.6 406.3 %all-gather.23.cloned.1.call-start = ((), (), s32[]{:S(2)}) async-start(), calls=%async_computation.15 | async-start | bytes 5898240 | tf_op jit(solution)/shard_map/all_gather | solution.py:282
  320.4 56.3 %copy-start.8 = (f32[256,1280]{1,0:T(8,128)}, f32[256,1280]{1,0:T(8,128)S(1)}, u32[]{:S(2)}) copy-start(f32[256,1280]{1,0:T(8,128)S(1)} %get-tuple-element.1033) | copy-start | bytes 3932164
  376.7 289.5 %reduce-scatter.9.cloned.1.call-start = ((), (), s32[]{:S(2)}) async-start(), calls=%async_computation.18 | async-start | bytes 8192000 | tf_op jit(solution)/shard_map/reduce_scatter | solution.py:306
  381.8 286.8 %reduce-scatter.7.cloned.1.call-start = ((), (), s32[]{:S(2)}) async-start(), calls=%async_computation.17 | async-start | bytes 8192000 | tf_op jit(solution)/shard_map/reduce_scatter | solution.py:305
  386.9 344.4 %reduce-scatter.11.cloned.1.call-start = ((), (), s32[]{:S(2)}) async-start(), calls=%async_computation.19 | async-start | bytes 8192000 | tf_op jit(solution)/shard_map/reduce_scatter | solution.py:307
  400.2 478.3 %reduce-scatter.5.cloned.1.call-start = ((), (), s32[]{:S(2)}) async-start(), calls=%async_computation.16 | async-start | bytes 24576000 | tf_op jit(solution)/shard_map/reduce_scatter | solution.py:304
  462.5 35.1 %copy-start.40 = (f32[256,16]{0,1:T(8,128)S(1)}, f32[256,16]{0,1:T(8,128)}, u32[]{:S(2)}) copy-start(f32[256,16]{0,1:T(8,128)} %get-tuple-element.1589) | copy-start | bytes 49156
  462.5 69.0 %copy-start.38 = (f32[1280]{0:T(1024)S(1)}, f32[1280]{0:T(1024)}, u32[]{:S(2)}) copy-start(f32[1280]{0:T(1024)} %copy-done.37) | copy-start | bytes 15364
  531.5 13.3 %copy-start.10 = (bf16[256,1280]{0,1:T(8,128)(2,1)S(1)}, bf16[256,1280]{0,1:T(8,128)(2,1)}, u32[]{:S(2)}) copy-start(bf16[256,1280]{0,1:T(8,128)(2,1)} %copy.95) | copy-start | bytes 1966084
  665.8 584.2 %all-reduce.12.cloned.1.call-start = ((), (), s32[]{:S(2)}) async-start(), calls=%async_computation.20 | async-start | bytes 19660800 | tf_op jit(solution)/shard_map/psum | solution.py:312
  885.6 72.0 %all-to-all-start.1 = ((f32[8,32,1280]{2,1,0:T(8,128)}), f32[8,32,1280]{2,1,0:T(8,128)S(1)}, u32[]{:S(2)}, u32[]{:S(2)}) async-start(f32[8,32,1280]{2,1,0:T(8,128)} %bitcast.281), calls=%async_computation.1 | async-start | bytes 2621440 | tf_op jit(solution)/shard_map/all_to_all | solution.py:316
  900.9 61.6 %copy-start.46 = (s32[256,1]{0,1:T(1,128)S(1)}, s32[256,1]{0,1:T(1,128)}, u32[]{:S(2)}) copy-start(s32[256,1]{0,1:T(1,128)} %copy-done.45) | copy-start | bytes 3076
  900.9 61.6 %copy-start.43 = (f32[1280]{0:T(1024)S(1)}, f32[1280]{0:T(1024)}, u32[]{:S(2)}) copy-start(f32[1280]{0:T(1024)} %get-tuple-element.1024) | copy-start | bytes 15364
  900.9 61.7 %copy-start.55 = (bf16[80]{0:T(256)(128)(2,1)S(1)}, bf16[80]{0:T(256)(128)(2,1)}, u32[]{:S(2)}) copy-start(bf16[80]{0:T(256)(128)(2,1)} %copy-done.54) | copy-start | bytes 484
  957.6 64.3 %all-to-all-start.3 = ((f32[8,32,1280]{2,1,0:T(8,128)}), f32[8,32,1280]{2,1,0:T(8,128)S(1)}, u32[]{:S(2)}, u32[]{:S(2)}) async-start(f32[8,32,1280]{2,1,0:T(8,128)} %bitcast.280), calls=%async_computation.3 | async-start | bytes 2621440 | tf_op jit(solution)/shard_map/all_to_all | solution.py:317
  (45 other events, 182.7 us)
Sparse Core Ops, SparseCore 0:
  9.6 69.5 all-gather.8
  89.1 100.2 all-gather.12
  191.6 84.4 all-gather.10
  277.4 27.4 all-gather.14
  306.4 29.3 all-gather.16
  337.1 29.2 all-gather.18
  368.6 86.2 all-gather.20
  457.1 87.7 all-gather.22
  547.4 58.4 reduce-scatter.8
  608.4 60.1 reduce-scatter.6
  671.1 60.0 reduce-scatter.10
  733.9 144.5 reduce-scatter.4
  882.9 367.0 all-reduce.11
where the time goes:
time: 1280 us; the launch traced here: 1270 us
  waiting for transfers between devices  705 us (55%)
  matrix products  193 us (15%)
  local copies, waits for them, and re-layouts  145 us (11%)
  blocking collectives  130 us (10%)
  other arithmetic  47.2 us (4%)
  starting transfers between devices  23.1 us (2%)
  between operations  17.8 us (1%)
    psum x1, waiting for transfers between devices, body(): lax.psum((owned[0], owned[1], owned[2], owned[3], owned[4], owned[5], own...  226 us
    reduce_scatter x1, waiting for transfers between devices, body(): lax.psum_scatter(grad_qkv, 'fsdp', scatter_dimension=0, tiled=True)  147 us
    reduce_scatter x1, waiting for transfers between devices, body(): lax.psum_scatter(grad_down, 'fsdp', scatter_dimension=0, tiled=True)  62.7 us
    dynamic_slice x22, local copies, waits for them, and re-layouts, in_blocks(): lax.scan(inner, carried, (jnp.arange(block_count, dtype=jnp.int32), split))  59.4 us
    all_to_all x1, waiting for transfers between devices, body(): lax.all_to_all(result[arrived_slot], 'ctx', split_axis=0, concat_axis=0,...  56.6 us
    dot_general x6, matrix products, pair_scores(): jnp.einsum('qhd,khd->qhk', left_rows.reshape(left_rows.shape[0], HEADS, -...  52.3 us
    all_gather x1, waiting for transfers between devices, body(): lax.all_gather(key_rows, 'ctx', axis=0, tiled=True)  50.5 us
    psum x1, blocking collectives, body(): lax.psum((owned[0], owned[1], owned[2], owned[3], owned[4], owned[5], own...  44.3 us
  transfers between devices with their start and end apart: 17, of which 14 were waited for; matrix products, arithmetic and copies ran while one was open for 28% of the time, Pallas kernels for 0%

commit v1 on v0

--- a/solution.py
+++ b/solution.py
@@ -1,8 +1,11 @@
+import functools
 import math
 
 import jax
 import jax.numpy as jnp
 from jax import lax
+from jax.experimental import pallas as pl
+from jax.experimental.pallas import tpu as pltpu
 from jax.sharding import PartitionSpec as P
 
 HEADS = 16
@@ -11,6 +14,80 @@
 EPS = 1e-06
 FLOOR = -1e30
 LOG2E = 1.442695041
+
+MESH = pl.DeviceIdType.MESH
+LANES = 128
+BF = jnp.bfloat16
+F32 = jnp.float32
+VMEM_SPEC = pl.BlockSpec(memory_space=pltpu.VMEM)
+VMEM_LIMIT = 60 << 20
+
+
+def flip(number, mask):
+    total = 0
+    for bit in (1, 2, 4):
+        left = (number // bit) % 2
+        right = (mask // bit) % 2
+        total = total + bit * (left + right - 2 * left * right)
+    return total
+
+
+class Place:
+    def __init__(self):
+        self.c = lax.axis_index("ctx")
+        self.f = lax.axis_index("fsdp")
+        self.core = self.f % 2
+        self.plane = self.f - self.core
+        self.half = self.c // 4
+        self.pack = self.plane + self.half
+        self.group = (self.c % 4) * 2 + self.core
+        self.twin = self.plane + 1 - self.core
+        self.across = (self.f + 2) % 4
+
+
+def dev(ctx, fsdp):
+    return {"ctx": ctx, "fsdp": fsdp}
+
+
+def send(src, dst, send_sem, recv_sem, device):
+    copy = pltpu.make_async_remote_copy(
+        src_ref=src,
+        dst_ref=dst,
+        send_sem=send_sem,
+        recv_sem=recv_sem,
+        device_id=device,
+        device_id_type=MESH,
+    )
+    copy.start()
+    return copy
+
+
+def await_recv(ref, sem):
+    pltpu.make_async_copy(ref, ref, sem).wait()
+
+
+def meet_plane(at):
+    barrier = pltpu.get_barrier_semaphore()
+
+    def greet(k, carry):
+        pl.semaphore_signal(
+            barrier,
+            1,
+            device_id=dev((at.c + k // 2) % 8, at.plane + (at.core + k) % 2),
+            device_id_type=MESH,
+        )
+        return carry
+
+    lax.fori_loop(1, 16, greet, 0)
+    for k in range(2):
+        pl.semaphore_signal(
+            barrier, 1, device_id=dev(at.c, (at.plane + 2) % 4 + k), device_id_type=MESH
+        )
+    pl.semaphore_wait(barrier, 17)
+
+
+def span(start, size, unit):
+    return pl.ds(pl.multiple_of(start, unit), size)
 
 
 def doc_index(places, seq_ends):
@@ -329,6 +406,879 @@
     )
 
 
+def attend_kernel(
+    x_ref,
+    w_ref,
+    aux_ref,
+    pos_ref,
+    att_ref,
+    normed_ref,
+    qkv_ref,
+    lse_ref,
+    out_ref,
+    auxsum_ref,
+    place_ref,
+    x_all,
+    w_all,
+    aux_all,
+    pos_all,
+    v_turned,
+    key_pos,
+    bias,
+    att_send,
+    x_send_sem,
+    x_recv_sem,
+    w_send_sem,
+    w_recv_sem,
+    aux_send_sem,
+    aux_recv_sem,
+    pos_sem,
+    att_send_sem,
+    att_recv_sem,
+    local_sem,
+):
+    at = Place()
+    meet_plane(at)
+    c, f = at.c, at.f
+    hub = at.core == at.half
+
+    w_own = pltpu.make_async_copy(
+        w_ref.at[at.core], w_all.at[span(f * 320, 320, 320)], local_sem.at[0]
+    )
+    w_own.start()
+    aux_own = pltpu.make_async_copy(aux_ref, aux_all.at[f], local_sem.at[1])
+    aux_own.start()
+    pos_own = pltpu.make_async_copy(pos_ref, pos_all.at[at.core], local_sem.at[2])
+    pos_own.start()
+    x_own = pltpu.make_async_copy(x_ref, x_all.at[c], local_sem.at[3])
+
+    x_far = pltpu.make_async_remote_copy(
+        src_ref=x_ref,
+        dst_ref=x_all.at[c],
+        send_sem=x_send_sem.at[0, 0],
+        recv_sem=x_recv_sem.at[c],
+        device_id=dev(flip(c, 4), f),
+        device_id_type=MESH,
+    )
+
+    @pl.when(hub)
+    def _():
+        x_own.start()
+        for k, where in enumerate((dev(flip(c, 1), f), dev(flip(c, 2), f), dev(c, at.twin))):
+            send(x_ref, x_all.at[c], x_send_sem.at[0, k], x_recv_sem.at[c], where)
+
+    @pl.when(jnp.logical_not(hub))
+    def _():
+        x_far.start()
+
+    w_copies, aux_copies = [], []
+    for k in (2, 1, 3):
+        to = (f + k) % 4
+        aux_copies.append(
+            send(
+                aux_ref,
+                aux_all.at[f],
+                aux_send_sem.at[k],
+                aux_recv_sem.at[f],
+                dev(c, to),
+            )
+        )
+        w_copies.append(
+            send(
+                w_ref.at[to % 2],
+                w_all.at[span(f * 320, 320, 320)],
+                w_send_sem.at[k],
+                w_recv_sem.at[f],
+                dev(c, to),
+            )
+        )
+    pos_copy = send(
+        pos_ref, pos_all.at[at.core], pos_sem.at[0], pos_sem.at[1], dev(c, at.twin)
+    )
+
+    aux_own.wait()
+    for k in (1, 2, 3):
+        await_recv(aux_all.at[0], aux_recv_sem.at[(f + k) % 4])
+    aux = jnp.zeros(aux_ref.shape, F32)
+    for k in range(4):
+        aux = aux + aux_all[k].astype(F32)
+    auxsum_ref[...] = aux
+    gain = aux[0:1, :]
+    scale = aux[2:3, :LANES]
+    real = lax.broadcasted_iota(jnp.int32, (1, LANES), 1) < 80
+    mult = jnp.where(
+        real, LOG2E / math.sqrt(80) * (jnp.maximum(scale, 0.0) + jnp.log1p(jnp.exp(-jnp.abs(scale)))), 0.0
+    )
+    one = jnp.ones_like(mult)
+    mults = jnp.concatenate([mult, mult, one, one, one, one], axis=1)
+
+    pos_own.wait()
+    await_recv(pos_all.at[0], pos_sem.at[1])
+    place_ref[...] = pos_all[at.half]
+    for k in range(8):
+        block = place_ref[0:1, k * 256 : (k + 1) * 256]
+        key_pos[k * 256 : (k + 1) * 256, :] = jnp.transpose(
+            jnp.broadcast_to(block, (256, 256))
+        )
+
+    def arrive(step, carry):
+        slot = flip(c, step)
+
+        @pl.when(jnp.logical_and(hub, step == 0))
+        def _():
+            x_own.wait()
+
+        @pl.when(jnp.logical_not(jnp.logical_and(hub, step == 0)))
+        def _():
+            await_recv(x_all.at[slot], x_recv_sem.at[slot])
+
+        def onward(way, where):
+            send(
+                x_all.at[slot],
+                x_all.at[slot],
+                x_send_sem.at[step, way],
+                x_recv_sem.at[slot],
+                where,
+            )
+
+        @pl.when(jnp.logical_and(hub, jnp.logical_or(step == 4, step == 6)))
+        def _():
+            onward(0, dev(flip(c, 1), f))
+
+        @pl.when(jnp.logical_and(hub, jnp.logical_or(step == 4, step == 1)))
+        def _():
+            onward(1, dev(flip(c, 2), f))
+
+        @pl.when(jnp.logical_and(hub, step > 0))
+        def _():
+            onward(2, dev(c, at.twin))
+
+        xf = x_all[slot].astype(F32)
+        inv = lax.rsqrt(jnp.mean(xf * xf, axis=1, keepdims=True) + EPS)
+        normed_ref[span(slot * 256, 256, 256), :] = (xf * inv * gain).astype(BF)
+        return carry
+
+    def project(step, carry):
+        slot = flip(c, step)
+        rows = span(slot * 256, 256, 256)
+        proj = jnp.dot(normed_ref[rows, :], w_all[...], preferred_element_type=F32)
+        qkv_ref[rows, :] = (proj * mults).astype(BF)
+        return carry
+
+    lax.fori_loop(0, 7, arrive, 0)
+    w_own.wait()
+    for k in (1, 2, 3):
+        await_recv(w_all.at[pl.ds(0, 320)], w_recv_sem.at[(f + k) % 4])
+    lax.fori_loop(0, 5, project, 0)
+    lax.fori_loop(7, 8, arrive, 0)
+    lax.fori_loop(5, 8, project, 0)
+
+    for h in range(2):
+        v_turned[h] = jnp.transpose(qkv_ref[:, (4 + h) * LANES : (5 + h) * LANES])
+
+    att_own = pltpu.make_async_copy(
+        att_send.at[c], att_ref.at[span(at.group * 160, 160, 160)], local_sem.at[3]
+    )
+
+    def att_copy(block):
+        return pltpu.make_async_remote_copy(
+            src_ref=att_send.at[block],
+            dst_ref=att_ref.at[span(at.group * 160, 160, 160)],
+            send_sem=att_send_sem.at[block],
+            recv_sem=att_recv_sem.at[at.group],
+            device_id=dev(block, at.pack),
+            device_id_type=MESH,
+        )
+
+    mine = at.core == at.half
+
+    def attend(step, carry):
+        block = flip(c, step)
+        lanes = span(block * 256, 256, 256)
+        high = place_ref[0:1, lanes]
+        least = place_ref[1:2, lanes]
+        kp = key_pos[...]
+        bias[...] = jnp.where((kp >= least) & (kp <= high), 0.0, FLOOR)
+        for h in range(2):
+            keys = qkv_ref[:, (2 + h) * LANES : (3 + h) * LANES]
+            query = qkv_ref[lanes, h * LANES : (h + 1) * LANES]
+            s = lax.dot_general(
+                keys, query, (((1,), (1,)), ((), ())), preferred_element_type=F32
+            )
+            s = s + bias[...]
+            top = jnp.max(s, axis=0, keepdims=True)
+            p = jnp.exp(s - top)
+            total = jnp.sum(p, axis=0, keepdims=True)
+            o = jnp.dot(v_turned[h], p.astype(BF), preferred_element_type=F32)
+            o = o[:80] / total
+            lse_ref[h : h + 1, lanes] = top + jnp.log(total)
+            out_ref[h * 80 : (h + 1) * 80, lanes] = o
+            att_send[block, h * 80 : (h + 1) * 80, :] = o.astype(BF)
+
+        @pl.when(jnp.logical_and(mine, step == 0))
+        def _():
+            att_own.start()
+
+        @pl.when(jnp.logical_not(jnp.logical_and(mine, step == 0)))
+        def _():
+            att_copy(block).start()
+
+        return carry
+
+    lax.fori_loop(0, 8, attend, 0)
+    for row in range(2, 8):
+        lse_ref[row : row + 1, :] = jnp.zeros((1, 2048), F32)
+
+    for copy in w_copies + aux_copies:
+        copy.wait_send()
+    pos_copy.wait_send()
+
+    @pl.when(hub)
+    def _():
+        for k in range(3):
+            await_recv(x_ref, x_send_sem.at[0, k])
+        for step in range(1, 8):
+            ways = {1: (1, 2), 4: (0, 1, 2), 6: (0, 2)}.get(step, (2,))
+            for way in ways:
+                await_recv(x_ref, x_send_sem.at[step, way])
+
+    @pl.when(jnp.logical_not(hub))
+    def _():
+        x_far.wait_send()
+
+    def finish(block, carry):
+        own = jnp.logical_and(mine, block == c)
+
+        @pl.when(own)
+        def _():
+            att_own.wait()
+
+        @pl.when(jnp.logical_not(own))
+        def _():
+            att_copy(block).wait_send()
+
+        own_in = jnp.logical_and(mine, block == at.group)
+
+        @pl.when(jnp.logical_not(own_in))
+        def _():
+            await_recv(att_ref.at[pl.ds(0, 160)], att_recv_sem.at[block])
+
+        return carry
+
+    lax.fori_loop(0, 8, finish, 0)
+
+
+def attend_forward(x, w_slices, aux, pos):
+    shape = jax.ShapeDtypeStruct
+    return pl.pallas_call(
+        attend_kernel,
+        name="attend_forward",
+        out_shape=(
+            shape((1280, 256), BF),
+            shape((2048, 1280), BF),
+            shape((2048, 768), BF),
+            shape((8, 2048), F32),
+            shape((160, 2048), F32),
+            shape((16, 1280), F32),
+            shape((8, 2048), F32),
+        ),
+        in_specs=[VMEM_SPEC] * 4,
+        out_specs=(VMEM_SPEC,) * 7,
+        scratch_shapes=[
+            pltpu.VMEM((8, 256, 1280), BF),
+            pltpu.VMEM((1280, 768), BF),
+            pltpu.VMEM((4, 16, 1280), BF),
+            pltpu.VMEM((2, 8, 2048), F32),
+            pltpu.VMEM((2, 128, 2048), BF),
+            pltpu.VMEM((2048, 256), F32),
+            pltpu.VMEM((2048, 256), F32),
+            pltpu.VMEM((8, 160, 256), BF),
+            pltpu.SemaphoreType.DMA((8, 3)),
+            pltpu.SemaphoreType.DMA((8,)),
+            pltpu.SemaphoreType.DMA((4,)),
+            pltpu.SemaphoreType.DMA((4,)),
+            pltpu.SemaphoreType.DMA((4,)),
+            pltpu.SemaphoreType.DMA((4,)),
+            pltpu.SemaphoreType.DMA((2,)),
+            pltpu.SemaphoreType.DMA((8,)),
+            pltpu.SemaphoreType.DMA((8,)),
+            pltpu.SemaphoreType.DMA((4,)),
+        ],
+        compiler_params=pltpu.CompilerParams(
+            collective_id=0, has_side_effects=True, vmem_limit_bytes=VMEM_LIMIT
+        ),
+        cost_estimate=pl.CostEstimate(
+            flops=14_000_000_000, bytes_accessed=40_000_000, transcendentals=8_400_000
+        ),
+    )(x, w_slices, aux, pos)
+
+
+def attend_grad_kernel(
+    grad_ref,
+    qkv_ref,
+    lse_ref,
+    out_ref,
+    place_ref,
+    normed_ref,
+    mult_ref,
+    back_ref,
+    weight_ref,
+    scale_ref,
+    grad_all,
+    key_pos,
+    bias,
+    k_turned,
+    delta,
+    key_sum,
+    value_sum,
+    turned,
+    g_send_sem,
+    g_recv_sem,
+    b_send_sem,
+    b_recv_sem,
+    local_sem,
+):
+    at = Place()
+    meet_plane(at)
+    c, f = at.c, at.f
+    mine = at.core == at.half
+
+    def grad_copy(group, h):
+        return pltpu.make_async_remote_copy(
+            src_ref=grad_ref.at[span(group * 160 + h * 80, 80, 80)],
+            dst_ref=grad_all.at[h, pl.ds(0, 80), span(c * 256, 256, 256)],
+            send_sem=g_send_sem.at[group, h],
+            recv_sem=g_recv_sem.at[c, h],
+            device_id=dev(at.core * 4 + group // 2, at.plane + group % 2),
+            device_id_type=MESH,
+        )
+
+    def grad_own(h):
+        return pltpu.make_async_copy(
+            grad_ref.at[span(at.group * 160 + h * 80, 80, 80)],
+            grad_all.at[h, pl.ds(0, 80), span(c * 256, 256, 256)],
+            local_sem.at[h],
+        )
+
+    def give(k, carry):
+        group = flip(at.group, k)
+
+        @pl.when(jnp.logical_and(mine, k == 0))
+        def _():
+            grad_own(0).start()
+            grad_own(1).start()
+
+        @pl.when(jnp.logical_not(jnp.logical_and(mine, k == 0)))
+        def _():
+            grad_copy(group, 0).start()
+            grad_copy(group, 1).start()
+
+        return carry
+
+    lax.fori_loop(0, 8, give, 0)
+
+    for h in range(2):
+        grad_all[h, 80:, :] = jnp.zeros((48, 2048), BF)
+        k_turned[h] = jnp.transpose(qkv_ref[:, (2 + h) * LANES : (3 + h) * LANES])
+    for k in range(8):
+        block = place_ref[0:1, k * 256 : (k + 1) * 256]
+        key_pos[k * 256 : (k + 1) * 256, :] = jnp.transpose(
+            jnp.broadcast_to(block, (256, 256))
+        )
+    scale_ref[...] = jnp.zeros((8, LANES), F32)
+
+    def take(k, carry):
+        block = flip(c, k)
+
+        @pl.when(jnp.logical_and(mine, k == 0))
+        def _():
+            grad_own(0).wait()
+            grad_own(1).wait()
+
+        @pl.when(jnp.logical_not(jnp.logical_and(mine, k == 0)))
+        def _():
+            for h in range(2):
+                await_recv(
+                    grad_all.at[h, pl.ds(0, 80), pl.ds(0, 256)], g_recv_sem.at[block, h]
+                )
+
+        return carry
+
+    lax.fori_loop(0, 8, take, 0)
+    for h in range(2):
+        delta[h : h + 1, :] = jnp.sum(
+            grad_all[h, :80, :].astype(F32) * out_ref[h * 80 : (h + 1) * 80, :],
+            axis=0,
+            keepdims=True,
+        )
+
+    for h in range(2):
+        key_sum[...] = jnp.zeros((2048, LANES), F32)
+        value_sum[...] = jnp.zeros((2048, LANES), F32)
+
+        def block_grad(block, carry, h=h):
+            lanes = span(block * 256, 256, 256)
+            high = place_ref[0:1, lanes]
+            least = place_ref[1:2, lanes]
+            kp = key_pos[...]
+            keys = qkv_ref[:, (2 + h) * LANES : (3 + h) * LANES]
+            values = qkv_ref[:, (4 + h) * LANES : (5 + h) * LANES]
+            query = qkv_ref[lanes, h * LANES : (h + 1) * LANES]
+            grad_t = grad_all[h, :, lanes]
+            s = lax.dot_general(
+                keys, query, (((1,), (1,)), ((), ())), preferred_element_type=F32
+            )
+            visible = (kp >= least) & (kp <= high)
+            p = jnp.exp(jnp.where(visible, s - lse_ref[h : h + 1, lanes], FLOOR))
+            gp = jnp.dot(values, grad_t, preferred_element_type=F32)
+            gs = (p * (gp - delta[h : h + 1, lanes])).astype(BF)
+            value_sum[...] += lax.dot_general(
+                p.astype(BF), grad_t, (((1,), (1,)), ((), ())), preferred_element_type=F32
+            )
+            key_sum[...] += jnp.dot(gs, query, preferred_element_type=F32)
+            q_grad = jnp.dot(k_turned[h], gs, preferred_element_type=F32)
+            scale_ref[0:1, :] += jnp.sum(
+                jnp.transpose(q_grad) * query.astype(F32), axis=0, keepdims=True
+            )
+            turned[h * 80 : (h + 1) * 80, lanes] = (
+                q_grad[:80] * mult_ref[:80, 0:1]
+            ).astype(BF)
+            return carry
+
+        lax.fori_loop(0, 8, block_grad, 0)
+        turned[160 + h * 80 : 160 + (h + 1) * 80, :] = jnp.transpose(key_sum[...])[:80].astype(BF)
+        turned[320 + h * 80 : 320 + (h + 1) * 80, :] = jnp.transpose(value_sum[...])[:80].astype(BF)
+
+    def back_copy(block, j):
+        return pltpu.make_async_remote_copy(
+            src_ref=turned.at[pl.ds(j * 160, 160), span(block * 256, 256, 256)],
+            dst_ref=back_ref.at[span(j * 1280 + at.group * 160, 160, 160)],
+            send_sem=b_send_sem.at[block, j],
+            recv_sem=b_recv_sem.at[at.group, j],
+            device_id=dev(block, at.pack),
+            device_id_type=MESH,
+        )
+
+    def back_own(j):
+        return pltpu.make_async_copy(
+            turned.at[pl.ds(j * 160, 160), span(c * 256, 256, 256)],
+            back_ref.at[span(j * 1280 + at.group * 160, 160, 160)],
+            local_sem.at[j],
+        )
+
+    def put(k, carry):
+        block = flip(c, k)
+
+        @pl.when(jnp.logical_and(mine, k == 0))
+        def _():
+            for j in range(3):
+                back_own(j).start()
+
+        @pl.when(jnp.logical_not(jnp.logical_and(mine, k == 0)))
+        def _():
+            for j in range(3):
+                back_copy(block, j).start()
+
+        return carry
+
+    lax.fori_loop(0, 8, put, 0)
+
+    for j in range(3):
+        weight_ref[j * 160 : (j + 1) * 160, :] = jnp.dot(
+            turned[j * 160 : (j + 1) * 160, :], normed_ref[...], preferred_element_type=F32
+        ).astype(BF)
+
+    def finish(block, carry):
+        own = jnp.logical_and(mine, block == c)
+
+        @pl.when(own)
+        def _():
+            for j in range(3):
+                back_own(j).wait()
+
+        @pl.when(jnp.logical_not(own))
+        def _():
+            for j in range(3):
+                back_copy(block, j).wait_send()
+
+        own_in = jnp.logical_and(mine, block == at.group)
+
+        @pl.when(jnp.logical_not(own_in))
+        def _():
+            for j in range(3):
+                await_recv(back_ref.at[pl.ds(0, 160)], b_recv_sem.at[block, j])
+            for h in range(2):
+                grad_copy(block, h).wait_send()
+
+        return carry
+
+    lax.fori_loop(0, 8, finish, 0)
+
+
+def attend_backward(grad_t, qkv, lse, out, place, normed, mult):
+    shape = jax.ShapeDtypeStruct
+    return pl.pallas_call(
+        attend_grad_kernel,
+        name="attend_backward",
+        out_shape=(shape((3840, 256), BF), shape((480, 1280), BF), shape((8, LANES), F32)),
+        in_specs=[VMEM_SPEC] * 7,
+        out_specs=(VMEM_SPEC,) * 3,
+        scratch_shapes=[
+            pltpu.VMEM((2, 128, 2048), BF),
+            pltpu.VMEM((2048, 256), F32),
+            pltpu.VMEM((8, 128), F32),
+            pltpu.VMEM((2, 128, 2048), BF),
+            pltpu.VMEM((8, 2048), F32),
+            pltpu.VMEM((2048, LANES), F32),
+            pltpu.VMEM((2048, LANES), F32),
+            pltpu.VMEM((480, 2048), BF),
+            pltpu.SemaphoreType.DMA((8, 2)),
+            pltpu.SemaphoreType.DMA((8, 2)),
+            pltpu.SemaphoreType.DMA((8, 3)),
+            pltpu.SemaphoreType.DMA((8, 3)),
+            pltpu.SemaphoreType.DMA((4,)),
+        ],
+        compiler_params=pltpu.CompilerParams(
+            collective_id=1, has_side_effects=True, vmem_limit_bytes=VMEM_LIMIT
+        ),
+        cost_estimate=pl.CostEstimate(
+            flops=24_000_000_000, bytes_accessed=40_000_000, transcendentals=8_400_000
+        ),
+    )(grad_t, qkv, lse, out, place, normed, mult)
+
+
+def add_rows(target, source, rows, step):
+    def one(k, carry):
+        part = span(k * step, step, step)
+        target[part, :] = (target[part, :].astype(F32) + source[part, :].astype(F32)).astype(
+            target.dtype
+        )
+        return carry
+
+    lax.fori_loop(0, rows // step, one, 0)
+
+
+def sum_rows(target, left, right, rows, step):
+    def one(k, carry):
+        part = span(k * step, step, step)
+        target[part, :] = (left[part, :].astype(F32) + right[part, :].astype(F32)).astype(
+            target.dtype
+        )
+        return carry
+
+    lax.fori_loop(0, rows // step, one, 0)
+
+
+def reduce_kernel(
+    first_ref,
+    second_ref,
+    third_ref,
+    slice_ref,
+    small_ref,
+    first_out,
+    second_out,
+    third_out,
+    slice_out,
+    small_out,
+    a0,
+    a1,
+    a2,
+    a3,
+    a4,
+    final,
+    s1,
+    s2,
+    small_in,
+    m_send,
+    m_recv,
+    q_send,
+    q_recv,
+    v_send,
+    v_recv,
+):
+    at = Place()
+    meet_plane(at)
+    c, f, core = at.c, at.f, at.core
+    row = f // 2
+    xbit, zbit, hbit = c % 2, (c // 2) % 2, c // 4
+    twin, across = dev(c, at.twin), dev(c, at.across)
+    xpeer, zpeer, hpeer = dev(flip(c, 1), f), dev(flip(c, 2), f), dev(flip(c, 4), f)
+    inputs = (first_ref, second_ref, third_ref)
+    outputs = (first_out, second_out, third_out)
+    copies = {}
+
+    def go(kind, stage, m, src, dst, where):
+        sems = {"m": (m_send, m_recv), "q": (q_send, q_recv), "v": (v_send, v_recv)}[kind]
+        copies[kind, stage, m] = send(
+            src, dst, sems[0].at[stage, m], sems[1].at[stage, m], where
+        )
+
+    def got(kind, stage, m):
+        copies[kind, stage, m].wait_recv()
+
+    half = xbit * 160
+    quarter = half + zbit * 80
+    side = span(hbit * 640, 640, 640)
+    other = span((1 - hbit) * 640, 640, 640)
+    k2 = zbit + 2 * xbit
+
+    def main(stage, m):
+        src = inputs[m]
+        if stage == 0:
+            for y in range(2):
+                go(
+                    "m", y, m, src.at[span((2 * y + 1 - core) * 320, 320, 320)],
+                    a0.at[m, y], twin,
+                )
+        if stage == 1:
+            for y in range(2):
+                got("m", y, m)
+                base = (2 * y + core) * 320
+                def one(k, carry, y=y, base=base):
+                    part = span(k * 80, 80, 80)
+                    a0[m, y, part, :] = (
+                        a0[m, y, part, :].astype(F32)
+                        + src[span(base + k * 80, 80, 80), :].astype(F32)
+                    ).astype(BF)
+                    return carry
+                lax.fori_loop(0, 4, one, 0)
+            go("m", 2, m, a0.at[m, 1 - row], a1.at[m], across)
+        if stage == 2:
+            got("m", 2, m)
+            add_rows(a1.at[m], a0.at[m, row], 320, 80)
+            go("m", 3, m, a1.at[m, span(160 - half, 160, 160)], a2.at[m], xpeer)
+        if stage == 3:
+            got("m", 3, m)
+            add_rows(a2.at[m], a1.at[m, span(half, 160, 160)], 160, 80)
+            go("m", 4, m, a2.at[m, span(80 - zbit * 80, 80, 80)], a3.at[m], zpeer)
+        if stage == 4:
+            got("m", 4, m)
+            add_rows(a3.at[m], a2.at[m, span(zbit * 80, 80, 80)], 80, 80)
+            go("m", 5, m, a3.at[m, :, other], a4.at[m], hpeer)
+        if stage == 5:
+            got("m", 5, m)
+            spot = span(quarter, 80, 80)
+            final[m, spot, side] = (
+                a4[m].astype(F32) + a3[m, :, side].astype(F32)
+            ).astype(BF)
+            piece = final.at[m, spot, side]
+            go("m", 6, m, piece, piece, hpeer)
+        if stage == 6:
+            got("m", 6, m)
+            piece = final.at[m, span(quarter, 80, 80)]
+            go("m", 7, m, piece, piece, zpeer)
+        if stage == 7:
+            got("m", 7, m)
+            piece = final.at[m, span(half, 160, 160)]
+            go("m", 8, m, piece, piece, xpeer)
+        if stage == 8:
+            got("m", 8, m)
+            outputs[m][...] = final[m].astype(F32)
+
+    def head(stage, j):
+        rows = pl.ds(j * 160, 160)
+        mine = slice_out.at[j, core]
+        if stage == 0:
+            go(
+                "q", 0, j, slice_ref.at[rows, span((1 - row) * 640, 640, 640)], s1.at[j], across
+            )
+        if stage == 1:
+            got("q", 0, j)
+            s1[j] = (
+                s1[j].astype(F32) + slice_ref[rows, span(row * 640, 640, 640)].astype(F32)
+            ).astype(BF)
+            go("q", 1, j, s1.at[j, span(80 - hbit * 80, 80, 80)], s2.at[j], hpeer)
+        if stage == 2:
+            got("q", 1, j)
+            own = span(hbit * 80, 80, 80)
+            slice_out[j, core, k2, own, :] = (
+                s2[j].astype(F32) + s1[j, own, :].astype(F32)
+            ).astype(BF)
+            piece = mine.at[k2, own]
+            go("q", 2, j, piece, piece, hpeer)
+        if stage == 3:
+            got("q", 2, j)
+            piece = mine.at[k2]
+            go("q", 3, j, piece, piece, zpeer)
+        if stage == 4:
+            got("q", 3, j)
+            piece = mine.at[pl.ds(2 * xbit, 2)]
+            go("q", 4, j, piece, piece, xpeer)
+        if stage == 5:
+            got("q", 4, j)
+            go("q", 5, j, mine, mine, twin)
+        if stage == 6:
+            got("q", 5, j)
+
+    def tiny(stage):
+        if stage > 0:
+            got("v", stage - 1, 0)
+            small_out[...] += small_in[stage - 1]
+        if stage < 5:
+            where = (twin, across, xpeer, zpeer, hpeer)[stage]
+            go("v", stage, 0, small_out, small_in.at[stage], where)
+
+    small_out[...] = small_ref[...]
+    for tick in range(12):
+        for m in range(3):
+            if 0 <= tick - m <= 6:
+                head(tick - m, m)
+        for m in range(3):
+            if 0 <= tick - m <= 8:
+                main(tick - m, m)
+        if tick < 6:
+            if tick > 0:
+                copies["v", tick - 1, 0].wait_send()
+            tiny(tick)
+    for key, copy in copies.items():
+        if key[0] != "v":
+            copy.wait_send()
+
+
+def reduce_grads(first, second, third, slices, small):
+    shape = jax.ShapeDtypeStruct
+    dma = pltpu.SemaphoreType.DMA
+    return pl.pallas_call(
+        reduce_kernel,
+        name="reduce_grads",
+        out_shape=(
+            shape((320, 1280), F32),
+            shape((320, 1280), F32),
+            shape((320, 1280), F32),
+            shape((3, 2, 4, 160, 640), BF),
+            shape((8, 1280), F32),
+        ),
+        in_specs=[VMEM_SPEC] * 5,
+        out_specs=(VMEM_SPEC,) * 5,
+        scratch_shapes=[
+            pltpu.VMEM((3, 2, 320, 1280), BF),
+            pltpu.VMEM((3, 320, 1280), BF),
+            pltpu.VMEM((3, 160, 1280), BF),
+            pltpu.VMEM((3, 80, 1280), BF),
+            pltpu.VMEM((3, 80, 640), BF),
+            pltpu.VMEM((3, 320, 1280), BF),
+            pltpu.VMEM((3, 160, 640), BF),
+            pltpu.VMEM((3, 80, 640), BF),
+            pltpu.VMEM((5, 8, 1280), F32),
+            dma((9, 3)),
+            dma((9, 3)),
+            dma((6, 3)),
+            dma((6, 3)),
+            dma((5, 1)),
+            dma((5, 1)),
+        ],
+        compiler_params=pltpu.CompilerParams(
+            collective_id=2, has_side_effects=True, vmem_limit_bytes=VMEM_LIMIT
+        ),
+        cost_estimate=pl.CostEstimate(flops=30_000_000, bytes_accessed=30_000_000, transcendentals=0),
+    )(first, second, third, slices, small)
+
+
+def fast_body(
+    tokens,
+    lengths,
+    position,
+    qkv_weight,
+    out_weight,
+    up_weight,
+    down_weight,
+    attn_gain,
+    mlp_gain,
+    query_scale,
+    cotangent,
+):
+    c, f = lax.axis_index("ctx"), lax.axis_index("fsdp")
+    x, dy = tokens[0], cotangent[0]
+    heads = qkv_weight.reshape(320, 3, HEADS, 80)
+    heads = lax.dynamic_slice_in_dim(heads, (c % 4) * 4, 4, 2)
+    heads = jnp.pad(heads, ((0, 0), (0, 0), (0, 0), (0, 48))).reshape(320, 3, 2, 2, LANES)
+    w_slices = heads.transpose(2, 0, 1, 3, 4).reshape(2, 320, 768)
+    aux = jnp.zeros((16, 1280), BF)
+    aux = lax.dynamic_update_slice(aux, attn_gain[None], (0, f * 320))
+    aux = lax.dynamic_update_slice(aux, mlp_gain[None], (1, f * 320))
+    aux = lax.dynamic_update_slice(aux, query_scale[None], (2, f * 20))
+    pos = position[0]
+    start = jnp.zeros_like(pos)
+    end = 0
+    for k in range(4):
+        end = end + lengths[0, k]
+        start = jnp.where(pos >= end, end, start)
+    places = jnp.concatenate([pos[None], start[None], jnp.zeros((6, 2048), jnp.int32)], axis=0)
+    places = places.astype(F32)
+
+    att_t, normed, qkv, lse, out, auxsum, place = attend_forward(x, w_slices, aux, places)
+
+    full_out, full_up, full_down, full_qkv = (
+        lax.all_gather(out_weight, "fsdp", axis=0, tiled=True),
+        lax.all_gather(up_weight, "fsdp", axis=0, tiled=True),
+        lax.all_gather(down_weight, "fsdp", axis=0, tiled=True),
+        lax.all_gather(qkv_weight, "fsdp", axis=0, tiled=True),
+    )
+    attn_gain_f, mlp_gain_f = auxsum[0], auxsum[1]
+    scale_float = auxsum[2, :80]
+    xf = x.astype(F32)
+    resid = xf + lax.dot_general(att_t, full_out, (((0,), (0,)), ((), ())), preferred_element_type=F32)
+    inv_mlp = lax.rsqrt(jnp.mean(resid * resid, axis=1, keepdims=True) + EPS)
+    normed_mlp = (resid * inv_mlp * mlp_gain_f).astype(BF)
+    up_proj = jnp.dot(normed_mlp, full_up, preferred_element_type=F32)
+    sigma = jax.nn.sigmoid(up_proj)
+    act_low = (up_proj * sigma).astype(BF)
+    result = resid + jnp.dot(act_low, full_down, preferred_element_type=F32)
+    grad_down = jnp.dot(act_low.T, dy, preferred_element_type=F32).astype(BF)
+    act_grad = jnp.dot(dy, full_down.T, preferred_element_type=F32)
+    up_grad = (act_grad * sigma * (1.0 + up_proj * (1.0 - sigma))).astype(BF)
+    grad_up = jnp.dot(normed_mlp.T, up_grad, preferred_element_type=F32).astype(BF)
+    norm_mlp_grad = jnp.dot(up_grad, full_up.T, preferred_element_type=F32)
+    grad_mlp_gain = jnp.sum(norm_mlp_grad * resid * inv_mlp, axis=0)
+    scaled_mlp = norm_mlp_grad * mlp_gain_f
+    resid_grad = dy.astype(F32) + inv_mlp * (
+        scaled_mlp - resid * inv_mlp * inv_mlp * jnp.mean(scaled_mlp * resid, axis=1, keepdims=True)
+    )
+    branch_grad = resid_grad.astype(BF)
+    grad_out = jnp.dot(att_t, branch_grad, preferred_element_type=F32).astype(BF)
+    grad_t = lax.dot_general(
+        full_out, branch_grad, (((1,), (1,)), ((), ())), preferred_element_type=F32
+    ).astype(BF)
+
+    base_scale = LOG2E / math.sqrt(80)
+    soft = jax.nn.softplus(scale_float)
+    mult = jnp.broadcast_to(jnp.pad(base_scale * soft, (0, 48))[:, None], (LANES, LANES))
+    back, slices, scale_sum = attend_backward(grad_t, qkv, lse, out, place, normed, mult)
+
+    inv_attn = lax.rsqrt(jnp.mean(xf * xf, axis=1, keepdims=True) + EPS)
+    norm_attn_grad = jnp.dot(full_qkv, back, preferred_element_type=F32).T
+    grad_attn_gain = jnp.sum(norm_attn_grad * xf * inv_attn, axis=0)
+    scaled_attn = norm_attn_grad * attn_gain_f
+    input_grad = resid_grad + inv_attn * (
+        scaled_attn - xf * inv_attn * inv_attn * jnp.mean(scaled_attn * xf, axis=1, keepdims=True)
+    )
+    grad_scale = scale_sum[0, :80] / soft * jax.nn.sigmoid(scale_float)
+    small = jnp.concatenate(
+        [
+            grad_attn_gain[None],
+            grad_mlp_gain[None],
+            jnp.pad(grad_scale, (0, 1200))[None],
+            jnp.zeros((5, 1280), F32),
+        ],
+        axis=0,
+    )
+    g_out, g_up, g_down, g_qkv, small = reduce_grads(grad_out, grad_up, grad_down, slices, small)
+    g_qkv = lax.dynamic_slice_in_dim(g_qkv, (f % 2) * 320, 320, 4)
+    g_qkv = g_qkv.reshape(3, 2, 2, 2, 160, 320).transpose(5, 0, 3, 2, 1, 4)
+    g_qkv = g_qkv.reshape(320, 3840).astype(F32)
+    return (
+        result[None],
+        input_grad[None],
+        g_qkv,
+        g_out,
+        g_up,
+        g_down,
+        lax.dynamic_slice_in_dim(small[0], f * 320, 320),
+        lax.dynamic_slice_in_dim(small[1], f * 320, 320),
+        lax.dynamic_slice_in_dim(small[2], f * 20, 20),
+    )
+
+
 def solution(mesh):
     placed = (
         P("fsdp", "ctx", None),
@@ -343,8 +1293,9 @@
         P("fsdp"),
         P("fsdp", "ctx", None),
     )
+    fits = mesh.shape["ctx"] == 8 and mesh.shape["fsdp"] == 4
     return jax.shard_map(
-        body,
+        fast_body if fits else body,
         mesh=mesh,
         in_specs=placed,
         out_specs=(

time: 1280 us -> 421 us (0.33)
  waiting for transfers between devices: 705 us -> 2.64 us
  Pallas kernels: 0 us -> 328 us
  matrix products: 193 us -> 33.1 us
  blocking collectives: 130 us -> 0 us
  local copies, waits for them, and re-layouts: 145 us -> 34.1 us
  other arithmetic: 47.2 us -> 5.58 us
  starting transfers between devices: 23.1 us -> 0.15 us
    pallas_call x0 -> x3, Pallas kernels: none -> 328 us  [the longest x1 151 us: reduce_grads(): pl.pallas_call(reduce_kernel, name='reduce_grads', out_shape=(shape((320,...]
    psum x1 -> x0, waiting for transfers between devices: 226 us -> none  [body(): lax.psum((owned[0], owned[1], owned[2], owned[3], owned[4], owned[5], own...]
    reduce_scatter x4 -> x0, waiting for transfers between devices: 212 us -> none  [the longest x1 147 us: body(): lax.psum_scatter(grad_qkv, 'fsdp', scatter_dimension=0, tiled=True)]
    all_gather x8 -> x4, waiting for transfers between devices: 166 us -> 0.06 us  [the longest x1 0.02 us: fast_body(): lax.all_gather(out_weight, 'fsdp', axis=0, tiled=True)]
    dot_general x26 -> x10, matrix products: 193 us -> 33.1 us  [the longest x1 7.34 us: fast_body(): norm_attn_grad = jnp.dot(full_qkv, back, preferred_element_type=F32).T]
    all_to_all x4 -> x0, waiting for transfers between devices: 98.1 us -> none  [the longest x1 56.6 us: body(): lax.all_to_all(result[arrived_slot], 'ctx', split_axis=0, concat_axis=0,...]
    all_gather x2 -> x0, blocking collectives: 67.1 us -> none  [the longest x1 33.9 us: body(): lax.all_gather(log_total, 'ctx', axis=0, tiled=True)]
    dynamic_slice x27 -> x4, local copies, waits for them, and re-layouts: 65.4 us -> 6.21 us  [the longest x1 3.76 us: fast_body(): g_qkv = lax.dynamic_slice_in_dim(g_qkv, f % 2 * 320, 320, 4)]
  transfers between devices with their start and end apart: 17 -> 4, of which waited for: 14 -> 0; matrix products, arithmetic and copies ran while one was open for 28% -> 9% of each run, Pallas kernels for 0% -> 42%
where the time goes in v1:
time: 421 us; the launch traced here: 420 us
  Pallas kernels  328 us (78%)
  local copies, waits for them, and re-layouts  34.1 us (8%)
  matrix products  33.1 us (8%)
  between operations  16.8 us (4%)
  other arithmetic  5.58 us (1%)
    pallas_call x1, Pallas kernels, reduce_grads(): pl.pallas_call(reduce_kernel, name='reduce_grads', out_shape=(shape((320,...  151 us
    pallas_call x1, Pallas kernels, attend_forward(): pl.pallas_call(attend_kernel, name='attend_forward', out_shape=(shape((12...  88.9 us
    pallas_call x1, Pallas kernels, attend_backward(): pl.pallas_call(attend_grad_kernel, name='attend_backward', out_shape=(sha...  87.7 us
    unnamed x45, local copies, waits for them, and re-layouts  17.6 us
  transfers between devices with their start and end apart: 4, of which 0 were waited for; matrix products, arithmetic and copies ran while one was open for 9% of the time, Pallas kernels for 42%

profile of v1, /device:TPU:0, one launch (start us, length us, event | category | flops | bytes accessed | tf_op | source)
XLA Modules:
  0.0 420.1 jit_solution(14202971334402531529)
XLA Ops:
  10.0 1.1 copy-done
  11.1 2.7 copy.22
  13.8 1.2 constant_dynamic-slice_fusion.2
  15.2 1.6 copy.24
  16.8 1.4 reshape.63.w_ref
  23.0 0.7 add_convert_fusion.pos_ref
  23.7 88.9 %attend_forward.1 = (bf16[1280,256]{1,0:T(8,128)(2,1)}, bf16[2048,1280]{1,0:T(8,128)(2,1)}, bf16[2048,768]{1,0:T(8,128)(2,1)}, f32[8,2048]{1,0:T(8,128)}, f32[16...) custom-call(bf16[256,1280]{1,0:T(8,128)(2,1)} %bitcast.78, bf16[2,320,768]{2,1,0:T(8,128)(2,1)} %reshape.63.w_ref, ...), custom_call_target="tpu_custom_call" | custom-call | flops 14000000000 | bytes 40000000 | tf_op jit(solution)/shard_map/attend_forward/pallas_call | solution.py:673
  113.4 0.9 slice_reduce_fusion
  114.6 3.3 multiply_reduce_fusion.2
  117.9 3.0 fusion.25
  120.9 4.3 %fusion.2 = bf16[256,1280]{1,0:T(8,128)(2,1)S(1)} fusion(bf16[1280,1280]{1,0:T(8,128)(2,1)} %all-gather.9.cloned.1.call-done, f32[256,1280]{1,0:T(8,128)S(1)} %fusion.25, bf16[1,256,1280]{2,1,0:T(8,128)(2,1)} %param.21), kind=kOutput, calls=%fused_computation.12 | convolution fusion | flops 841809920 | bytes 5898240 | tf_op jit(solution)/shard_map/dot_general | solution.py:1228
  125.6 1.2 multiply_reduce_fusion
  127.5 1.8 copy-done.19
  129.3 1.9 fusion.3.grad_ref
  131.2 0.7 broadcast_in_dim.59.mult_ref
  131.9 87.7 %attend_backward.1 = (bf16[3840,256]{1,0:T(8,128)(2,1)}, bf16[480,1280]{1,0:T(8,128)(2,1)}, f32[8,128]{1,0:T(8,128)}) custom-call(bf16[1280,256]{1,0:T(8,128)(2,1)} %fusion.3.grad_ref, bf16[2048,768]{1,0:T(8,128)(2,1)} %get-tuple-element.26.qkv_ref, f32[8,2048]{1,0:T(8,128)} %get-tuple-element.27.lse_ref, f32[160,2048]{1,0:T(8,128)} %get-tuple-element.28.out_ref, ...), custom_call_target="tpu_custom_call" | custom-call | flops 24000000000 | bytes 40000000 | tf_op jit(solution)/shard_map/attend_backward/pallas_call | solution.py:920
  220.4 3.9 convolution_convert_fusion.2.first_ref
  224.2 2.9 convolution_convert_fusion.1.second_ref
  227.2 3.0 convolution_convert_fusion.third_ref
  230.2 2.3 fusion.1
  232.5 7.3 %fusion.13 = (f32[1280]{0:T(1024)S(1)}, f32[256]{0:T(256)S(1)}, f32[256,1280]{1,0:T(8,128)S(1)}) fusion(f32[256]{0:T(256)S(1)} %add_rsqrt_fusion, bf16[1,256,1280]{2,1,0:T(8,128)(2,1)S(1)} %copy-done.2, f32[1280]{0:T(1024)S(1)} %get-tuple-element.52, bf16[3840,256]{1,0:T(8,128)(2,1)} %get-tuple-element.31, bf16[1280,3840]{1,0:T(8,128)(2,1)} %all-gather.11.cloned.1.call-done), kind=kOutput, calls=%fused_computation.24 | convolution fusion | flops 2518874624 | bytes 13774848 | tf_op jit(solution)/shard_map/dot_general | solution.py:1249
  240.5 151.1 %reduce_grads.1 = (f32[320,1280]{1,0:T(8,128)}, f32[320,1280]{1,0:T(8,128)}, f32[320,1280]{1,0:T(8,128)}, bf16[3,2,4,160,640]{4,3,2,1,0:T(8,128)(2,1)}, f32[8,1280]{1,0:T(8,128)}) custom-call(bf16[1280,1280]{1,0:T(8,128)(2,1)} %convolution_convert_fusion.2.first_ref, bf16[1280,1280]{1,0:T(8,128)(2,1)} %convolution_convert_fusion.1.second_ref, ...), custom_call_target="tpu_custom_call" | custom-call | flops 30000000 | bytes 30000000 | tf_op jit(solution)/shard_map/reduce_grads/pallas_call | solution.py:1141
  391.7 3.8 constant_dynamic-slice_fusion.1
  395.4 3.2 copy.26
  398.7 6.1 %copy.27 = f32[320,3840]{1,0:T(8,128)} copy(f32[320,3840]{0,1:T(8,128)} %bitcast.74) | data formatting | bytes 9830400
  404.8 0.9 fusion.26
  406.2 1.5 fusion.10
  408.4 1.2 copy.36
  409.5 0.9 copy-done.4
  410.4 1.2 copy.37
  411.6 0.9 copy-done.3
  412.4 1.2 copy.38
  (77 shorter events, 9.7 us)
Async XLA Ops:
  7.2 107.4 %all-gather.5.cloned.1.call-start = ((), (), s32[]{:S(2)}) async-start(), calls=%async_computation | async-start | bytes 4096000 | tf_op jit(solution)/shard_map/all_gather | solution.py:1212
  7.9 110.0 %all-gather.7.cloned.1.call-start = ((), (), s32[]{:S(2)}) async-start(), calls=%async_computation.1 | async-start | bytes 4096000 | tf_op jit(solution)/shard_map/all_gather | solution.py:1213
  8.7 112.3 %all-gather.9.cloned.1.call-start = ((), (), s32[]{:S(2)}) async-start(), calls=%async_computation.2 | async-start | bytes 4096000 | tf_op jit(solution)/shard_map/all_gather | solution.py:1214
  9.4 1.7 copy-start
  9.4 223.0 %all-gather.11.cloned.1.call-start = ((), (), s32[]{:S(2)}) async-start(), calls=%async_computation.3 | async-start | bytes 12288000 | tf_op jit(solution)/shard_map/all_gather | solution.py:1215
  16.8 1.5 copy-start.15
  16.8 1.5 copy-start.16
  16.8 2.0 copy-start.14
  16.8 5.3 %copy-start.17 = (bf16[20]{0:T(256)(128)(2,1)S(1)}, bf16[20]{0:T(256)(128)(2,1)}, u32[]{:S(2)}) copy-start(bf16[20]{0:T(256)(128)(2,1)} %param.20) | copy-start | bytes 124
  16.8 5.4 %copy-start.13 = (s32[1,2048]{1,0:T(1,128)S(1)}, s32[1,2048]{1,0:T(1,128)}, u32[]{:S(2)}) copy-start(s32[1,2048]{1,0:T(1,128)} %param.13) | copy-start | bytes 24580
  22.3 1.4 copy-start.12
  23.7 90.6 %copy-start.2 = (bf16[1,256,1280]{2,1,0:T(8,128)(2,1)S(1)}, bf16[1,256,1280]{2,1,0:T(8,128)(2,1)}, u32[]{:S(2)}) copy-start(bf16[1,256,1280]{2,1,0:T(8,128)(2,1)} %param.11) | copy-start | bytes 1966084
  120.9 4.3 %copy-start.6 = (f32[256,1280]{1,0:T(8,128)}, f32[256,1280]{1,0:T(8,128)S(1)}, u32[]{:S(2)}) copy-start(f32[256,1280]{1,0:T(8,128)S(1)} %fusion.25) | copy-start | bytes 3932164
  120.9 4.7 %copy-start.1 = (bf16[1280,1280]{1,0:T(8,128)(2,1)S(1)}, bf16[1280,1280]{1,0:T(8,128)(2,1)}, u32[]{:S(2)}) copy-start(bf16[1280,1280]{1,0:T(8,128)(2,1)} %all-gather.7.cloned.1.call-done) | copy-start | bytes 9830404
  125.6 1.2 copy-start.10
  125.6 1.5 copy-start.8
  127.1 2.2 copy-start.19
  220.3 3.9 copy-start.11
  224.2 2.9 copy-start.7
  224.2 2.9 copy-start.9
  227.2 3.0 copy-start.18
  406.2 2.1 copy-start.5
  408.4 2.0 copy-start.4
  410.4 2.0 copy-start.3
Sparse Core Ops, SparseCore 0:
  9.6 37.5 all-gather.4
  48.8 33.1 all-gather.6
  83.5 29.7 all-gather.8
  114.7 66.4 all-gather.10

commit v2 on v0

--- a/solution.py
+++ b/solution.py
@@ -1,8 +1,11 @@
+import functools
 import math
 
 import jax
 import jax.numpy as jnp
 from jax import lax
+from jax.experimental import pallas as pl
+from jax.experimental.pallas import tpu as pltpu
 from jax.sharding import PartitionSpec as P
 
 HEADS = 16
@@ -11,6 +14,80 @@
 EPS = 1e-06
 FLOOR = -1e30
 LOG2E = 1.442695041
+
+MESH = pl.DeviceIdType.MESH
+LANES = 128
+BF = jnp.bfloat16
+F32 = jnp.float32
+VMEM_SPEC = pl.BlockSpec(memory_space=pltpu.VMEM)
+VMEM_LIMIT = 60 << 20
+
+
+def flip(number, mask):
+    total = 0
+    for bit in (1, 2, 4):
+        left = (number // bit) % 2
+        right = (mask // bit) % 2
+        total = total + bit * (left + right - 2 * left * right)
+    return total
+
+
+class Place:
+    def __init__(self):
+        self.c = lax.axis_index("ctx")
+        self.f = lax.axis_index("fsdp")
+        self.core = self.f % 2
+        self.plane = self.f - self.core
+        self.half = self.c // 4
+        self.pack = self.plane + self.half
+        self.group = (self.c % 4) * 2 + self.core
+        self.twin = self.plane + 1 - self.core
+        self.across = (self.f + 2) % 4
+
+
+def dev(ctx, fsdp):
+    return {"ctx": ctx, "fsdp": fsdp}
+
+
+def send(src, dst, send_sem, recv_sem, device):
+    copy = pltpu.make_async_remote_copy(
+        src_ref=src,
+        dst_ref=dst,
+        send_sem=send_sem,
+        recv_sem=recv_sem,
+        device_id=device,
+        device_id_type=MESH,
+    )
+    copy.start()
+    return copy
+
+
+def await_recv(ref, sem):
+    pltpu.make_async_copy(ref, ref, sem).wait()
+
+
+def meet_plane(at):
+    barrier = pltpu.get_barrier_semaphore()
+
+    def greet(k, carry):
+        pl.semaphore_signal(
+            barrier,
+            1,
+            device_id=dev((at.c + k // 2) % 8, at.plane + (at.core + k) % 2),
+            device_id_type=MESH,
+        )
+        return carry
+
+    lax.fori_loop(1, 16, greet, 0)
+    for k in range(2):
+        pl.semaphore_signal(
+            barrier, 1, device_id=dev(at.c, (at.plane + 2) % 4 + k), device_id_type=MESH
+        )
+    pl.semaphore_wait(barrier, 17)
+
+
+def span(start, size, unit):
+    return pl.ds(pl.multiple_of(start, unit), size)
 
 
 def doc_index(places, seq_ends):
@@ -329,6 +406,1099 @@
     )
 
 
+def attend_kernel(
+    ends_ref,
+    x_ref,
+    w_ref,
+    aux_ref,
+    pos_ref,
+    out_w_ref,
+    up_w_ref,
+    down_w_ref,
+    dy_ref,
+    att_ref,
+    normed_ref,
+    qkv_ref,
+    lse_ref,
+    out_ref,
+    auxsum_ref,
+    place_ref,
+    w_all,
+    result_ref,
+    resid_grad_ref,
+    branch_ref,
+    up_grad_ref,
+    act_ref,
+    normed_mlp_ref,
+    grad_ref,
+    x_all,
+    w_own,
+    weights,
+    aux_all,
+    pos_all,
+    v_turned,
+    key_pos,
+    bias,
+    att_send,
+    x_send_sem,
+    x_recv_sem,
+    w_send_sem,
+    w_recv_sem,
+    aux_send_sem,
+    aux_recv_sem,
+    pos_sem,
+    att_send_sem,
+    att_recv_sem,
+    m_send_sem,
+    m_recv_sem,
+    local_sem,
+):
+    at = Place()
+    meet_plane(at)
+    c, f = at.c, at.f
+    hub = at.core == at.half
+
+    aux_own = pltpu.make_async_copy(aux_ref, aux_all.at[f], local_sem.at[1])
+    aux_own.start()
+    x_own = pltpu.make_async_copy(x_ref, x_all.at[c], local_sem.at[3])
+
+    x_far = pltpu.make_async_remote_copy(
+        src_ref=x_ref,
+        dst_ref=x_all.at[c],
+        send_sem=x_send_sem.at[0, 0],
+        recv_sem=x_recv_sem.at[c],
+        device_id=dev(flip(c, 4), f),
+        device_id_type=MESH,
+    )
+
+    @pl.when(hub)
+    def _():
+        x_own.start()
+        for k, where in enumerate((dev(flip(c, 1), f), dev(flip(c, 2), f), dev(c, at.twin))):
+            send(x_ref, x_all.at[c], x_send_sem.at[0, k], x_recv_sem.at[c], where)
+
+    @pl.when(jnp.logical_not(hub))
+    def _():
+        x_far.start()
+
+    w_copies, aux_copies = [], []
+    for k in (2, 1, 3):
+        aux_copies.append(
+            send(
+                aux_ref,
+                aux_all.at[f],
+                aux_send_sem.at[k],
+                aux_recv_sem.at[f],
+                dev(c, (f + k) % 4),
+            )
+        )
+
+    pos = pos_ref[...]
+    start = jnp.zeros_like(pos)
+    end = 0
+    for k in range(4):
+        end = end + ends_ref[0, k]
+        start = jnp.where(pos >= end, end, start)
+    pos_all[at.core, 0:1, :] = pos.astype(F32)
+    pos_all[at.core, 1:2, :] = start.astype(F32)
+    pos_all[at.core, 2:8, :] = jnp.zeros((6, 2048), F32)
+    pos_copy = send(
+        pos_all.at[at.core], pos_all.at[at.core], pos_sem.at[0], pos_sem.at[1], dev(c, at.twin)
+    )
+
+    row = lax.broadcasted_iota(jnp.int32, (1280, 512), 0)
+    column = lax.broadcasted_iota(jnp.int32, (1280, 512), 1)
+    inside = column % LANES
+    wanted = (c % 4) * 320 + column // LANES * 80 + inside
+    pick = jnp.where((row == wanted) & (inside < 80), 1.0, 0.0).astype(BF)
+    for j in range(3):
+        some = jnp.dot(w_ref[:, j * 1280 : (j + 1) * 1280], pick, preferred_element_type=F32)
+        for k in range(2):
+            w_own[k, :, j * 256 : (j + 1) * 256] = some[:, k * 256 : (k + 1) * 256].astype(BF)
+    mine_rows = span(f * 320, 320, 320)
+    for k in (2, 3, 1):
+        to = (f + k) % 4
+        w_copies.append(
+            send(
+                w_own.at[to % 2],
+                w_all.at[mine_rows],
+                w_send_sem.at[k],
+                w_recv_sem.at[f],
+                dev(c, to),
+            )
+        )
+    w_all[mine_rows, :] = w_own[at.core]
+
+    shards = (out_w_ref, up_w_ref, down_w_ref)
+    xbit = c % 2
+    other = (f + 2) % 4
+
+    def part(m, owner, x):
+        return weights.at[m, span(owner * 320 + x * 160, 160, 160)]
+
+    def weight_copy(m, way):
+        if way == 0:
+            src, dst, to = shards[m], weights.at[m, mine_rows], dev(c, at.twin)
+        elif way == 1:
+            src = shards[m].at[span(xbit * 160, 160, 160)]
+            dst, to = part(m, f, xbit), dev(c, other)
+        else:
+            x = (xbit, xbit, 1 - xbit)[way - 2]
+            src = dst = part(m, other, x)
+            to = (dev(flip(c, 1), f), dev(c, at.twin), dev(c, at.twin))[way - 2]
+        return pltpu.make_async_remote_copy(
+            src_ref=src,
+            dst_ref=dst,
+            send_sem=m_send_sem.at[m, way],
+            recv_sem=m_recv_sem.at[m, way],
+            device_id=to,
+            device_id_type=MESH,
+        )
+
+    def weight_first(m):
+        weight_copy(m, 0).start()
+        weight_copy(m, 1).start()
+        weights[m, mine_rows, :] = shards[m][...]
+
+    def weight_second(m):
+        weight_copy(m, 1).wait_recv()
+        weight_copy(m, 2).start()
+        weight_copy(m, 3).start()
+
+    def weight_third(m):
+        weight_copy(m, 2).wait_recv()
+        weight_copy(m, 4).start()
+
+    def weight_last(m):
+        for way in (0, 3, 4):
+            weight_copy(m, way).wait_recv()
+
+    weight_first(0)
+
+    aux_own.wait()
+    for k in (1, 2, 3):
+        await_recv(aux_all.at[0], aux_recv_sem.at[(f + k) % 4])
+    aux = jnp.zeros((16, 1280), F32)
+    scale = jnp.zeros((16, LANES), F32)
+    row = lax.broadcasted_iota(jnp.int32, (384, 1280), 0)
+    column = lax.broadcasted_iota(jnp.int32, (384, 1280), 1)
+    for k in range(4):
+        put = jnp.where((column == row + k * 320) & (row < 320), 1.0, 0.0).astype(BF)
+        aux = aux + jnp.dot(aux_all[k], put, preferred_element_type=F32)
+        put = (column[:LANES, :LANES] == row[:LANES, :LANES] + k * 20) & (row[:LANES, :LANES] < 20)
+        put = jnp.where(put, 1.0, 0.0).astype(BF)
+        scale = scale + jnp.dot(aux_all[k, :, :LANES], put, preferred_element_type=F32)
+    auxsum_ref[...] = aux
+    auxsum_ref[2:3, :LANES] = scale[2:3]
+    gain = aux[0:1, :]
+    mlp_gain = aux[1:2, :]
+    scale = scale[2:3]
+    real = lax.broadcasted_iota(jnp.int32, (1, LANES), 1) < 80
+    mult = jnp.where(
+        real, LOG2E / math.sqrt(80) * (jnp.maximum(scale, 0.0) + jnp.log1p(jnp.exp(-jnp.abs(scale)))), 0.0
+    )
+    one = jnp.ones_like(mult)
+    mults = jnp.concatenate([mult, mult, one, one, one, one], axis=1)
+
+    await_recv(pos_all.at[0], pos_sem.at[1])
+    place_ref[...] = pos_all[at.half]
+    for k in range(8):
+        block = place_ref[0:1, k * 256 : (k + 1) * 256]
+        key_pos[k * 256 : (k + 1) * 256, :] = jnp.transpose(
+            jnp.broadcast_to(block, (256, 256))
+        )
+
+    def arrive(step, carry):
+        slot = flip(c, step)
+
+        @pl.when(jnp.logical_and(hub, step == 0))
+        def _():
+            x_own.wait()
+
+        @pl.when(jnp.logical_not(jnp.logical_and(hub, step == 0)))
+        def _():
+            await_recv(x_all.at[slot], x_recv_sem.at[slot])
+
+        def onward(way, where):
+            send(
+                x_all.at[slot],
+                x_all.at[slot],
+                x_send_sem.at[step, way],
+                x_recv_sem.at[slot],
+                where,
+            )
+
+        @pl.when(jnp.logical_and(hub, jnp.logical_or(step == 4, step == 6)))
+        def _():
+            onward(0, dev(flip(c, 1), f))
+
+        @pl.when(jnp.logical_and(hub, jnp.logical_or(step == 4, step == 1)))
+        def _():
+            onward(1, dev(flip(c, 2), f))
+
+        @pl.when(jnp.logical_and(hub, step > 0))
+        def _():
+            onward(2, dev(c, at.twin))
+
+        xf = x_all[slot].astype(F32)
+        inv = lax.rsqrt(jnp.mean(xf * xf, axis=1, keepdims=True) + EPS)
+        normed_ref[span(slot * 256, 256, 256), :] = (xf * inv * gain).astype(BF)
+        return carry
+
+    def project(step, carry):
+        slot = flip(c, step)
+        rows = span(slot * 256, 256, 256)
+        proj = jnp.dot(normed_ref[rows, :], w_all[...], preferred_element_type=F32)
+        qkv_ref[rows, :] = (proj * mults).astype(BF)
+        return carry
+
+    lax.fori_loop(0, 7, arrive, 0)
+    for k in (1, 2, 3):
+        await_recv(w_all.at[pl.ds(0, 320)], w_recv_sem.at[(f + k) % 4])
+    weight_first(1)
+    weight_first(2)
+    weight_second(0)
+    lax.fori_loop(0, 5, project, 0)
+    lax.fori_loop(7, 8, arrive, 0)
+    lax.fori_loop(5, 8, project, 0)
+
+    for h in range(2):
+        v_turned[h] = jnp.transpose(qkv_ref[:, (4 + h) * LANES : (5 + h) * LANES])
+
+    att_own = pltpu.make_async_copy(
+        att_send.at[c], att_ref.at[span(at.group * 160, 160, 160)], local_sem.at[3]
+    )
+
+    def att_copy(block):
+        return pltpu.make_async_remote_copy(
+            src_ref=att_send.at[block],
+            dst_ref=att_ref.at[span(at.group * 160, 160, 160)],
+            send_sem=att_send_sem.at[block],
+            recv_sem=att_recv_sem.at[at.group],
+            device_id=dev(block, at.pack),
+            device_id_type=MESH,
+        )
+
+    mine = at.core == at.half
+
+    def attend(step, carry):
+        block = flip(c, step)
+        lanes = span(block * 256, 256, 256)
+        high = place_ref[0:1, lanes]
+        least = place_ref[1:2, lanes]
+        kp = key_pos[...]
+        bias[...] = jnp.where((kp >= least) & (kp <= high), 0.0, FLOOR)
+        for h in range(2):
+            keys = qkv_ref[:, (2 + h) * LANES : (3 + h) * LANES]
+            query = qkv_ref[lanes, h * LANES : (h + 1) * LANES]
+            s = lax.dot_general(
+                keys, query, (((1,), (1,)), ((), ())), preferred_element_type=F32
+            )
+            s = s + bias[...]
+            top = jnp.max(s, axis=0, keepdims=True)
+            p = jnp.exp(s - top)
+            total = jnp.sum(p, axis=0, keepdims=True)
+            o = jnp.dot(v_turned[h], p.astype(BF), preferred_element_type=F32)
+            o = o[:80] / total
+            lse_ref[h : h + 1, lanes] = top + jnp.log(total)
+            out_ref[h * 80 : (h + 1) * 80, lanes] = o.astype(BF)
+            att_send[block, h * 80 : (h + 1) * 80, :] = o.astype(BF)
+
+        @pl.when(jnp.logical_and(mine, step == 0))
+        def _():
+            att_own.start()
+
+        @pl.when(jnp.logical_not(jnp.logical_and(mine, step == 0)))
+        def _():
+            att_copy(block).start()
+
+        for when, todo in ((1, weight_third), (4, weight_second), (6, weight_second), (7, weight_third)):
+            m = {(1, weight_third): 0, (4, weight_second): 1, (6, weight_second): 2}.get((when, todo), 1)
+
+            @pl.when(step == when)
+            def _(todo=todo, m=m):
+                todo(m)
+
+        return carry
+
+    lax.fori_loop(0, 8, attend, 0)
+    lse_ref[2:8, :] = jnp.zeros((6, 2048), F32)
+
+    def land(block, carry):
+        @pl.when(jnp.logical_not(jnp.logical_and(mine, block == at.group)))
+        def _():
+            await_recv(att_ref.at[pl.ds(0, 160)], att_recv_sem.at[block])
+
+        return carry
+
+    @pl.when(mine)
+    def _():
+        att_own.wait()
+
+    weight_last(0)
+    lax.fori_loop(0, 8, land, 0)
+
+    def across(left, right):
+        return lax.dot_general(
+            left, right, (((1,), (1,)), ((), ())), preferred_element_type=F32
+        )
+
+    xf = x_ref[...].astype(F32)
+    resid = xf + jnp.dot(jnp.transpose(att_ref[...]), weights[0], preferred_element_type=F32)
+    inv = lax.rsqrt(jnp.mean(resid * resid, axis=1, keepdims=True) + EPS)
+    normed_mlp = (resid * inv * mlp_gain).astype(BF)
+    normed_mlp_ref[...] = jnp.transpose(normed_mlp)
+    weight_third(2)
+    weight_last(1)
+    up = jnp.dot(normed_mlp, weights[1], preferred_element_type=F32)
+    sigma = 1.0 / (1.0 + jnp.exp(-up))
+    act = (up * sigma).astype(BF)
+    act_ref[...] = jnp.transpose(act)
+    slope = sigma * (1.0 + up * (1.0 - sigma))
+    weight_last(2)
+    dy = dy_ref[...]
+    up_grad = (across(dy, weights[2]) * slope).astype(BF)
+    up_grad_ref[...] = up_grad
+    scaled = across(up_grad, weights[1]) * mlp_gain
+    resid_grad = dy.astype(F32) + inv * (
+        scaled - resid * inv * inv * jnp.mean(scaled * resid, axis=1, keepdims=True)
+    )
+    resid_grad_ref[...] = resid_grad
+    branch = resid_grad.astype(BF)
+    branch_ref[...] = branch
+    grad_ref[...] = across(weights[0], branch).astype(BF)
+    result_ref[...] = resid + jnp.dot(act, weights[2], preferred_element_type=F32)
+
+    for copy in w_copies + aux_copies:
+        copy.wait_send()
+    pos_copy.wait_send()
+    for m in range(3):
+        for way in range(5):
+            weight_copy(m, way).wait_send()
+
+    @pl.when(hub)
+    def _():
+        for k in range(3):
+            await_recv(x_ref, x_send_sem.at[0, k])
+        for step in range(1, 8):
+            ways = {1: (1, 2), 4: (0, 1, 2), 6: (0, 2)}.get(step, (2,))
+            for way in ways:
+                await_recv(x_ref, x_send_sem.at[step, way])
+
+    @pl.when(jnp.logical_not(hub))
+    def _():
+        x_far.wait_send()
+
+    def finish(block, carry):
+        @pl.when(jnp.logical_not(jnp.logical_and(mine, block == c)))
+        def _():
+            att_copy(block).wait_send()
+
+        return carry
+
+    lax.fori_loop(0, 8, finish, 0)
+
+
+def forward(*args):
+    shape = jax.ShapeDtypeStruct
+    dma = pltpu.SemaphoreType.DMA
+    return pl.pallas_call(
+        attend_kernel,
+        name="forward",
+        out_shape=(
+            shape((1280, 256), BF),
+            shape((2048, 1280), BF),
+            shape((2048, 768), BF),
+            shape((8, 2048), F32),
+            shape((160, 2048), BF),
+            shape((16, 1280), F32),
+            shape((8, 2048), F32),
+            shape((1280, 768), BF),
+            shape((256, 1280), F32),
+            shape((256, 1280), F32),
+            shape((256, 1280), BF),
+            shape((256, 1280), BF),
+            shape((1280, 256), BF),
+            shape((1280, 256), BF),
+            shape((1280, 256), BF),
+        ),
+        in_specs=[pl.BlockSpec(memory_space=pltpu.SMEM)] + [VMEM_SPEC] * 8,
+        out_specs=(VMEM_SPEC,) * 15,
+        scratch_shapes=[
+            pltpu.VMEM((8, 256, 1280), BF),
+            pltpu.VMEM((2, 320, 768), BF),
+            pltpu.VMEM((3, 1280, 1280), BF),
+            pltpu.VMEM((4, 16, 384), BF),
+            pltpu.VMEM((2, 8, 2048), F32),
+            pltpu.VMEM((2, 128, 2048), BF),
+            pltpu.VMEM((2048, 256), F32),
+            pltpu.VMEM((2048, 256), F32),
+            pltpu.VMEM((8, 160, 256), BF),
+            dma((8, 3)),
+            dma((8,)),
+            dma((4,)),
+            dma((4,)),
+            dma((4,)),
+            dma((4,)),
+            dma((2,)),
+            dma((8,)),
+            dma((8,)),
+            dma((3, 5)),
+            dma((3, 5)),
+            dma((4,)),
+        ],
+        compiler_params=pltpu.CompilerParams(
+            collective_id=0, has_side_effects=True, vmem_limit_bytes=VMEM_LIMIT
+        ),
+        cost_estimate=pl.CostEstimate(
+            flops=20_000_000_000, bytes_accessed=40_000_000, transcendentals=8_400_000
+        ),
+    )(*args)
+
+
+def add_into(target, source, rows, step):
+    def one(k, carry):
+        part = span(k * step, step, step)
+        target[part, :] = (target[part, :].astype(F32) + source[part, :].astype(F32)).astype(BF)
+        return carry
+
+    lax.fori_loop(0, rows // step, one, 0)
+
+
+KEY_PARTS = 2
+KEY_ROWS = 2048 // KEY_PARTS
+
+
+def backward_kernel(
+    grad_ref,
+    att_ref,
+    branch_ref,
+    normed_mlp_ref,
+    up_grad_ref,
+    act_ref,
+    dy_ref,
+    qkv_ref,
+    lse_ref,
+    out_ref,
+    place_ref,
+    normed_hbm,
+    w_ref,
+    mult_ref,
+    x_ref,
+    resid_grad_ref,
+    gain_ref,
+    first_out,
+    second_out,
+    third_out,
+    slice_out,
+    input_grad_ref,
+    scale_ref,
+    grad_all,
+    key_pos,
+    k_turned,
+    delta,
+    key_sum,
+    value_sum,
+    turned,
+    normed_part,
+    n_core,
+    n_x,
+    n_z,
+    n_last,
+    sums,
+    a0,
+    a1,
+    a2,
+    a3,
+    a4,
+    slices,
+    s1,
+    s2,
+    gathered,
+    strip,
+    scale_in,
+    g_send_sem,
+    g_recv_sem,
+    local_sem,
+    m_send,
+    m_recv,
+    q_send,
+    q_recv,
+    nc_send,
+    nc_recv,
+    n_send,
+    n_recv,
+    v_send,
+    v_recv,
+):
+    at = Place()
+    meet_plane(at)
+    c, f, core, half = at.c, at.f, at.core, at.half
+    mine = core == half
+    row = f // 2
+    xbit, zbit = c % 2, (c // 2) % 2
+    twin, across = dev(c, at.twin), dev(c, at.across)
+    xpeer, zpeer, hpeer = dev(flip(c, 1), f), dev(flip(c, 2), f), dev(flip(c, 4), f)
+
+    def remote(src, dst, send_sem, recv_sem, where):
+        return pltpu.make_async_remote_copy(
+            src_ref=src,
+            dst_ref=dst,
+            send_sem=send_sem,
+            recv_sem=recv_sem,
+            device_id=where,
+            device_id_type=MESH,
+        )
+
+    def grad_copy(group, h):
+        return remote(
+            grad_ref.at[span(group * 160 + h * 80, 80, 80)],
+            grad_all.at[h, pl.ds(0, 80), span(c * 256, 256, 256)],
+            g_send_sem.at[group, h],
+            g_recv_sem.at[c, h],
+            dev(core * 4 + group // 2, at.plane + group % 2),
+        )
+
+    def grad_own(h):
+        return pltpu.make_async_copy(
+            grad_ref.at[span(at.group * 160 + h * 80, 80, 80)],
+            grad_all.at[h, pl.ds(0, 80), span(c * 256, 256, 256)],
+            local_sem.at[h],
+        )
+
+    def give(k, carry):
+        group = flip(at.group, k)
+
+        @pl.when(jnp.logical_and(mine, k == 0))
+        def _():
+            grad_own(0).start()
+            grad_own(1).start()
+
+        @pl.when(jnp.logical_not(jnp.logical_and(mine, k == 0)))
+        def _():
+            grad_copy(group, 0).start()
+            grad_copy(group, 1).start()
+
+        return carry
+
+    lax.fori_loop(0, 8, give, 0)
+
+    side, other = span(half * 640, 640, 640), span(640 - half * 640, 640, 640)
+    quarter = xbit * 160 + zbit * 80
+    results = (first_out, second_out, third_out)
+
+    def main_copy(stage, m):
+        if stage < 2:
+            rows = pl.ds((m * 2 + stage) * 320, 320)
+            ends = sums.at[rows], a0.at[m, stage], twin
+        elif stage == 2:
+            ends = a0.at[m, 1 - row], a1.at[m], across
+        elif stage == 3:
+            ends = a1.at[m, span(160 - xbit * 160, 160, 160)], a2.at[m], xpeer
+        elif stage == 4:
+            ends = a2.at[m, span(80 - zbit * 80, 80, 80)], a3.at[m], zpeer
+        elif stage == 5:
+            ends = a3.at[m, :, other], a4.at[m], hpeer
+        else:
+            if stage == 6:
+                piece, to = results[m].at[span(quarter, 80, 80), side], hpeer
+            elif stage == 7:
+                piece, to = results[m].at[span(quarter, 80, 80)], zpeer
+            else:
+                piece, to = results[m].at[span(xbit * 160, 160, 160)], xpeer
+            ends = piece, piece, to
+        return remote(ends[0], ends[1], m_send.at[stage, m], m_recv.at[stage, m], ends[2])
+
+    def main(stage, m):
+        if stage == 0:
+            main_copy(0, m).start()
+            main_copy(1, m).start()
+            return
+        if stage == 1:
+            for y in range(2):
+                main_copy(y, m).wait_recv()
+                a0[m, y] = (a0[m, y].astype(F32) + weight_rows(m, 2 * y + core)).astype(BF)
+            return
+        if stage > 2:
+            main_copy(stage - 1, m).wait_recv()
+        if stage == 3:
+            add_into(a1.at[m], a0.at[m, row], 320, 80)
+        if stage == 4:
+            add_into(a2.at[m], a1.at[m, span(xbit * 160, 160, 160)], 160, 80)
+        if stage == 5:
+            add_into(a3.at[m], a2.at[m, span(zbit * 80, 80, 80)], 80, 80)
+        if stage == 6:
+            results[m][span(quarter, 80, 80), side] = (
+                a4[m].astype(F32) + a3[m, :, side].astype(F32)
+            ).astype(BF)
+        if stage < 9:
+            main_copy(stage, m).start()
+
+    lefts = (act_ref, normed_mlp_ref, att_ref)
+    rights = (dy_ref, up_grad_ref, branch_ref)
+
+    def weight_rows(m, quarter):
+        rows = span(quarter * 320, 320, 320)
+        return jnp.dot(lefts[m][rows, :], rights[m][...], preferred_element_type=F32)
+
+    for m in range(3):
+        for y in range(2):
+            part = weight_rows(m, 2 * y + 1 - core)
+            sums[(m * 2 + y) * 320 : (m * 2 + y + 1) * 320, :] = part.astype(BF)
+        main(0, m)
+    main(1, 0)
+    main(2, 0)
+
+    for h in range(2):
+        grad_all[h, 80:, :] = jnp.zeros((48, 2048), BF)
+        k_turned[h] = jnp.transpose(qkv_ref[:, (2 + h) * LANES : (3 + h) * LANES])
+    for k in range(8):
+        block = place_ref[0:1, k * 256 : (k + 1) * 256]
+        key_pos[k * 256 : (k + 1) * 256, :] = jnp.transpose(
+            jnp.broadcast_to(block, (LANES, 256))
+        )
+    scale_ref[...] = jnp.zeros((8, LANES), F32)
+    main(1, 1)
+
+    def take(k, carry):
+        block = flip(c, k)
+
+        @pl.when(jnp.logical_and(mine, k == 0))
+        def _():
+            grad_own(0).wait()
+            grad_own(1).wait()
+
+        @pl.when(jnp.logical_not(jnp.logical_and(mine, k == 0)))
+        def _():
+            for h in range(2):
+                await_recv(
+                    grad_all.at[h, pl.ds(0, 80), pl.ds(0, 256)], g_recv_sem.at[block, h]
+                )
+
+        return carry
+
+    lax.fori_loop(0, 8, take, 0)
+    main(1, 2)
+    for h in range(2):
+        delta[h : h + 1, :] = jnp.sum(
+            grad_all[h, :80, :].astype(F32) * out_ref[h * 80 : (h + 1) * 80, :].astype(F32),
+            axis=0,
+            keepdims=True,
+        )
+
+    place4 = zbit + 2 * xbit
+
+    def head_copy(stage, h):
+        if stage == 0:
+            ends = slices.at[h, :, span((1 - row) * 640, 640, 640)], s1.at[h], across
+        elif stage == 1:
+            ends = s1.at[h, span(128 - half * 128, 128, 128)], s2.at[h], hpeer
+        else:
+            if stage == 2:
+                piece, to = gathered.at[core, place4, h, span(half * 128, 128, 128)], hpeer
+            elif stage == 3:
+                piece, to = gathered.at[core, place4, h], zpeer
+            elif stage == 4:
+                piece, to = gathered.at[core, pl.ds(2 * xbit, 2), h], xpeer
+            else:
+                piece, to = gathered.at[core, :, h], twin
+            ends = piece, piece, to
+        return remote(ends[0], ends[1], q_send.at[stage, h], q_recv.at[stage, h], ends[2])
+
+    def head(stage, h):
+        if stage > 0:
+            head_copy(stage - 1, h).wait_recv()
+        if stage == 1:
+            add_into(s1.at[h], slices.at[h, :, span(row * 640, 640, 640)], 256, 128)
+        if stage == 2:
+            own = span(half * 128, 128, 128)
+            gathered[core, place4, h, own, :] = (
+                s2[h].astype(F32) + s1[h, own, :].astype(F32)
+            ).astype(BF)
+        if stage < 6:
+            head_copy(stage, h).start()
+
+    hooks = {
+        (0, 4): (lambda: main(2, 1),),
+        (0, 6): (lambda: main(3, 0),),
+        (1, 0): (lambda: main(4, 0),),
+        (1, 1): (lambda: main(5, 0),),
+        (1, 2): (lambda: main(6, 0), lambda: main(2, 2)),
+        (1, 3): (lambda: main(7, 0),),
+        (1, 4): (lambda: main(8, 0), lambda: main(3, 1)),
+        (1, 5): (lambda: head(1, 0), lambda: main(4, 1)),
+        (1, 6): (lambda: head(2, 0), lambda: main(5, 1)),
+        (1, 7): (lambda: head(3, 0), lambda: main(6, 1)),
+    }
+
+    def normed_load(part):
+        return pltpu.make_async_copy(
+            normed_hbm.at[:, pl.ds(part * 256, 256)], normed_part.at[part % 2], local_sem.at[2 + part % 2]
+        )
+
+    normed_load(0).start()
+    for h in range(2):
+        key_sum[...] = jnp.zeros((2048, LANES), F32)
+        value_sum[...] = jnp.zeros((2048, LANES), F32)
+
+        def block_grad(block, carry, h=h):
+            lanes = span(block * 256, 256, 256)
+            high = place_ref[0:1, lanes]
+            least = place_ref[1:2, lanes]
+            query = qkv_ref[lanes, h * LANES : (h + 1) * LANES]
+            grad_t = grad_all[h, :, lanes]
+            q_grad = jnp.zeros((LANES, 256), F32)
+            for part in range(KEY_PARTS):
+                some = slice(part * KEY_ROWS, (part + 1) * KEY_ROWS)
+                kp = key_pos[some, :]
+                kp = jnp.concatenate([kp, kp], axis=1)
+                keys = qkv_ref[some, (2 + h) * LANES : (3 + h) * LANES]
+                values = qkv_ref[some, (4 + h) * LANES : (5 + h) * LANES]
+                s = lax.dot_general(
+                    keys, query, (((1,), (1,)), ((), ())), preferred_element_type=F32
+                )
+                visible = (kp >= least) & (kp <= high)
+                p = jnp.exp(jnp.where(visible, s - lse_ref[h : h + 1, lanes], FLOOR))
+                gp = jnp.dot(values, grad_t, preferred_element_type=F32)
+                gs = (p * (gp - delta[h : h + 1, lanes])).astype(BF)
+                value_sum[some, :] += lax.dot_general(
+                    p.astype(BF), grad_t, (((1,), (1,)), ((), ())), preferred_element_type=F32
+                )
+                key_sum[some, :] += jnp.dot(gs, query, preferred_element_type=F32)
+                q_grad += jnp.dot(k_turned[h, :, some], gs, preferred_element_type=F32)
+            scale_ref[0:1, :] += jnp.sum(
+                jnp.transpose(q_grad) * query.astype(F32), axis=0, keepdims=True
+            )
+            turned[h * LANES : (h + 1) * LANES, lanes] = (q_grad * mult_ref[:, 0:1]).astype(BF)
+            for (hh, step), todo in hooks.items():
+                if hh == h:
+
+                    @pl.when(block == step)
+                    def _(todo=todo):
+                        for one in todo:
+                            one()
+
+            return carry
+
+        lax.fori_loop(0, 8, block_grad, 0)
+        for j, total in ((1, key_sum), (2, value_sum)):
+            low = jnp.transpose(total[...]).astype(BF)
+            turned[(2 * j + h) * LANES : (2 * j + h + 1) * LANES, :] = low
+        slices[h, 240:, :] = jnp.zeros((16, 1280), BF)
+        for part in range(5):
+            normed_load(part).wait()
+            if part + 1 < 5:
+                normed_load(part + 1).start()
+            for j in range(3):
+                first = (2 * j + h) * LANES
+                slices[h, j * 80 : (j + 1) * 80, part * 256 : (part + 1) * 256] = jnp.dot(
+                    turned[first : first + 80, :],
+                    normed_part[part % 2],
+                    preferred_element_type=F32,
+                ).astype(BF)
+        if h == 0:
+            normed_load(0).start()
+        head(0, h)
+
+    def norm_bits(k):
+        return (1 - xbit, 1 - xbit, xbit, xbit)[k], (1 - zbit, zbit, 1 - zbit, zbit)[k]
+
+    def norm_spot(k, hh):
+        slot = 2 * k + hh
+        return sums.at[pl.ds(slot // 5 * 640, 640), pl.ds(slot % 5 * 256, 256)]
+
+    def norm_copy(stage, k, hh=0):
+        if stage == 0:
+            return remote(
+                norm_spot(k, hh), n_core.at[k, hh], nc_send.at[k, hh], nc_recv.at[k, hh], twin
+            )
+        took = k
+        if stage == 1:
+            ends = n_core.at[k], n_x.at[k], xpeer
+        elif stage == 2:
+            ends = n_core.at[2, (1 - half, half)[k]], n_z.at[k], zpeer
+        else:
+            to = dev(flip(c, 4), at.pack) if k == 0 else dev(c, at.twin)
+            took = (core, 2)[k]
+            ends = n_core.at[3, (1 - half, half)[k]], n_last.at[core], to
+        return remote(ends[0], ends[1], n_send.at[stage, k], n_recv.at[stage, took], ends[2])
+
+    def norm_part(k, hh, which):
+        xs, zs = norm_bits(k)
+        lanes = span((hh * 4 + zs * 2 + xs) * 256, 256, 256)
+        rows = span(which * 640, 640, 640)
+        return jnp.dot(w_ref[rows, :], turned[:, lanes], preferred_element_type=F32)
+
+    for m in range(3):
+        for stage in range(2):
+            main_copy(stage, m).wait_send()
+    for k in range(4):
+        for hh in range(2):
+            norm_spot(k, hh)[...] = norm_part(k, hh, 1 - core).astype(BF)
+            norm_copy(0, k, hh).start()
+
+    def norm_core(k):
+        for hh in range(2):
+            norm_copy(0, k, hh).wait_recv()
+            n_core[k, hh] = (n_core[k, hh].astype(F32) + norm_part(k, hh, core)).astype(BF)
+
+    for k in range(2):
+        norm_core(k)
+        norm_copy(1, k).start()
+    head(1, 1)
+    norm_core(2)
+    norm_core(3)
+
+    def scale_copy(stage):
+        where = (twin, across, xpeer, zpeer, hpeer)[stage]
+        return remote(scale_ref, scale_in.at[stage], v_send.at[stage], v_recv.at[stage], where)
+
+    def tiny(stage):
+        if stage > 0:
+            scale_copy(stage - 1).wait()
+            scale_ref[...] += scale_in[stage - 1]
+        if stage < 5:
+            scale_copy(stage).start()
+
+    tiny(0)
+    main(7, 1)
+    head(4, 0)
+    main(3, 2)
+    head(2, 1)
+    tiny(1)
+    main(8, 1)
+    head(5, 0)
+    main(4, 2)
+    norm_copy(1, 0).wait_recv()
+    for hh in range(2):
+        add_into(n_core.at[2, hh], n_x.at[0, hh], 640, 80)
+    norm_copy(2, 0).start()
+    norm_copy(2, 1).start()
+    tiny(2)
+    head(3, 1)
+    main(5, 2)
+    norm_copy(1, 1).wait_recv()
+    for hh in range(2):
+        add_into(n_core.at[3, hh], n_x.at[1, hh], 640, 80)
+    tiny(3)
+    main(6, 2)
+    norm_copy(2, 0).wait_recv()
+    add_into(n_core.at[3, 1 - half], n_z.at[0], 640, 80)
+    norm_copy(3, 0).start()
+    norm_copy(2, 1).wait_recv()
+    add_into(n_core.at[3, half], n_z.at[1], 640, 80)
+
+    @pl.when(jnp.logical_not(mine))
+    def _():
+        norm_copy(3, 1).start()
+
+    tiny(4)
+    main(7, 2)
+    head(4, 1)
+    main(8, 2)
+    tiny(5)
+
+    @pl.when(mine)
+    def _():
+        n_last[core] = n_core[3, half]
+        await_recv(n_last.at[0], n_recv.at[3, 2])
+
+    @pl.when(jnp.logical_not(mine))
+    def _():
+        await_recv(n_last.at[0], n_recv.at[3, 0])
+        await_recv(n_last.at[1], n_recv.at[3, 1])
+
+    xf = x_ref[...].astype(F32)
+    inv = lax.rsqrt(jnp.mean(xf * xf, axis=1, keepdims=True) + EPS)
+    scaled = jnp.concatenate(
+        [jnp.transpose(n_last[k].astype(F32)) for k in range(2)], axis=1
+    ) * gain_ref[0:1, :]
+    input_grad_ref[...] = resid_grad_ref[...] + inv * (
+        scaled - xf * inv * inv * jnp.mean(scaled * xf, axis=1, keepdims=True)
+    )
+    for m in range(3):
+        main(9, m)
+    head(6, 0)
+    head(5, 1)
+    head(6, 1)
+    for k in range(4):
+        for hh in range(2):
+            norm_copy(0, k, hh).wait_send()
+    for core_k in range(2):
+        for m4 in range(4):
+            group = 2 * (2 * (m4 % 2) + m4 // 2) + core_k
+            for h in range(2):
+                for j in range(3):
+                    start = j * 1280 + (group * 2 + h) * 80
+                    sums[
+                        start % 1920 : start % 1920 + 80, start // 1920 * 640 : start // 1920 * 640 + 640
+                    ] = gathered[core_k, m4, h, j * 80 : (j + 1) * 80, :]
+
+    for part in range(2):
+
+        def turn(k, carry, part=part):
+            strip[...] = jnp.transpose(sums[span(k * LANES, LANES, LANES), part * 640 : part * 640 + 640])
+            slice_out[:, span(part * 1920 + k * LANES, LANES, LANES)] = strip[span(core * 320, 320, 320), :]
+            return carry
+
+        lax.fori_loop(0, 15, turn, 0)
+
+    def sent(block, carry):
+        own_in = jnp.logical_and(mine, block == at.group)
+
+        @pl.when(jnp.logical_not(own_in))
+        def _():
+            for h in range(2):
+                grad_copy(block, h).wait_send()
+
+        return carry
+
+    lax.fori_loop(0, 8, sent, 0)
+    for m in range(3):
+        for stage in range(2, 9):
+            main_copy(stage, m).wait_send()
+    for h in range(2):
+        for stage in range(6):
+            head_copy(stage, h).wait_send()
+    for k in range(2):
+        norm_copy(1, k).wait_send()
+        norm_copy(2, k).wait_send()
+    norm_copy(3, 0).wait_send()
+
+    @pl.when(jnp.logical_not(mine))
+    def _():
+        norm_copy(3, 1).wait_send()
+
+
+def backward(*args):
+    shape = jax.ShapeDtypeStruct
+    dma = pltpu.SemaphoreType.DMA
+    specs = [VMEM_SPEC] * 17
+    specs[11] = pl.BlockSpec(memory_space=pl.ANY)
+    return pl.pallas_call(
+        backward_kernel,
+        name="backward",
+        out_shape=(
+            shape((320, 1280), BF),
+            shape((320, 1280), BF),
+            shape((320, 1280), BF),
+            shape((320, 3840), BF),
+            shape((256, 1280), F32),
+            shape((8, LANES), F32),
+        ),
+        in_specs=specs,
+        out_specs=(VMEM_SPEC,) * 6,
+        scratch_shapes=[
+            pltpu.VMEM((2, 128, 2048), BF),
+            pltpu.VMEM((2048, LANES), F32),
+            pltpu.VMEM((2, 128, 2048), BF),
+            pltpu.VMEM((8, 2048), F32),
+            pltpu.VMEM((2048, LANES), F32),
+            pltpu.VMEM((2048, LANES), F32),
+            pltpu.VMEM((768, 2048), BF),
+            pltpu.VMEM((2, 2048, 256), BF),
+            pltpu.VMEM((4, 2, 640, 256), BF),
+            pltpu.VMEM((2, 2, 640, 256), BF),
+            pltpu.VMEM((2, 640, 256), BF),
+            pltpu.VMEM((2, 640, 256), BF),
+            pltpu.VMEM((1920, 1280), BF),
+            pltpu.VMEM((3, 2, 320, 1280), BF),
+            pltpu.VMEM((3, 320, 1280), BF),
+            pltpu.VMEM((3, 160, 1280), BF),
+            pltpu.VMEM((3, 80, 1280), BF),
+            pltpu.VMEM((3, 80, 640), BF),
+            pltpu.VMEM((2, 256, 1280), BF),
+            pltpu.VMEM((2, 256, 640), BF),
+            pltpu.VMEM((2, 128, 640), BF),
+            pltpu.VMEM((2, 4, 2, 256, 640), BF),
+            pltpu.VMEM((640, LANES), BF),
+            pltpu.VMEM((5, 8, LANES), F32),
+            dma((8, 2)),
+            dma((8, 2)),
+            dma((4,)),
+            dma((9, 3)),
+            dma((9, 3)),
+            dma((6, 2)),
+            dma((6, 2)),
+            dma((4, 2)),
+            dma((4, 2)),
+            dma((4, 4)),
+            dma((4, 4)),
+            dma((5,)),
+            dma((5,)),
+        ],
+        compiler_params=pltpu.CompilerParams(
+            collective_id=1, has_side_effects=True, vmem_limit_bytes=VMEM_LIMIT
+        ),
+        cost_estimate=pl.CostEstimate(
+            flops=30_000_000_000, bytes_accessed=60_000_000, transcendentals=8_400_000
+        ),
+    )(*args)
+
+
+def fast_body(
+    tokens,
+    lengths,
+    position,
+    qkv_weight,
+    out_weight,
+    up_weight,
+    down_weight,
+    attn_gain,
+    mlp_gain,
+    query_scale,
+    cotangent,
+):
+    f = lax.axis_index("fsdp")
+    x, dy = tokens[0], cotangent[0]
+    small = [jnp.pad(a, (0, 384 - a.shape[0])) for a in (attn_gain, mlp_gain, query_scale)]
+    small = jnp.stack(small + [jnp.zeros((384,), BF)] * 13)
+    (
+        att_t, normed, qkv, lse, out, auxsum, place, w_heads,
+        result, resid_grad, branch_grad, up_grad, act_t, normed_mlp_t, grad_t,
+    ) = forward(
+        lengths, x, qkv_weight, small, position, out_weight, up_weight, down_weight, dy
+    )
+    scale_float = auxsum[2, :80]
+    base_scale = LOG2E / math.sqrt(80)
+    soft = jax.nn.softplus(scale_float)
+    mult = jnp.broadcast_to(jnp.pad(base_scale * soft, (0, 48))[:, None], (LANES, LANES))
+    g_down, g_up, g_out, g_qkv, input_grad, scale_sum = backward(
+        grad_t,
+        att_t,
+        branch_grad,
+        normed_mlp_t,
+        up_grad,
+        act_t,
+        dy,
+        qkv,
+        lse,
+        out,
+        place,
+        normed,
+        w_heads,
+        mult,
+        x,
+        resid_grad,
+        auxsum,
+    )
+    g_down, g_up, g_out, g_qkv = (g.astype(F32) for g in (g_down, g_up, g_out, g_qkv))
+    grad_attn_gain = jnp.sum(qkv_weight.astype(F32) * g_qkv, axis=1) / attn_gain.astype(F32)
+    grad_mlp_gain = jnp.sum(up_weight.astype(F32) * g_up, axis=1) / mlp_gain.astype(F32)
+    grad_scale = scale_sum[0, :80] / soft * jax.nn.sigmoid(scale_float)
+    return (
+        result[None],
+        input_grad[None],
+        g_qkv,
+        g_out,
+        g_up,
+        g_down,
+        grad_attn_gain,
+        grad_mlp_gain,
+        lax.dynamic_slice_in_dim(grad_scale, f * 20, 20),
+    )
+
+
 def solution(mesh):
     placed = (
         P("fsdp", "ctx", None),
@@ -343,8 +1513,9 @@
         P("fsdp"),
         P("fsdp", "ctx", None),
     )
+    fits = mesh.shape["ctx"] == 8 and mesh.shape["fsdp"] == 4
     return jax.shard_map(
-        body,
+        fast_body if fits else body,
         mesh=mesh,
         in_specs=placed,
         out_specs=(

time: 1280 us -> 350 us (0.27)
  waiting for transfers between devices: 705 us -> 0 us
  Pallas kernels: 0 us -> 328 us
  matrix products: 193 us -> 0 us
  local copies, waits for them, and re-layouts: 145 us -> 7.44 us
  blocking collectives: 130 us -> 0 us
  other arithmetic: 47.2 us -> 10.5 us
  starting transfers between devices: 23.1 us -> 0 us
  between operations: 17.8 us -> 0.72 us
    pallas_call x0 -> x2, Pallas kernels: none -> 328 us  [the longest x1 220 us: backward(): pl.pallas_call(backward_kernel, name='backward', out_shape=(shape((320, 1...]
    psum x1 -> x0, waiting for transfers between devices: 226 us -> none  [body(): lax.psum((owned[0], owned[1], owned[2], owned[3], owned[4], owned[5], own...]
    reduce_scatter x4 -> x0, waiting for transfers between devices: 212 us -> none  [the longest x1 147 us: body(): lax.psum_scatter(grad_qkv, 'fsdp', scatter_dimension=0, tiled=True)]
    dot_general x26 -> x0, matrix products: 193 us -> none  [the longest x6 52.3 us: pair_scores(): jnp.einsum('qhd,khd->qhk', left_rows.reshape(left_rows.shape[0], HEADS, -...]
    all_gather x8 -> x0, waiting for transfers between devices: 166 us -> none  [the longest x1 50.5 us: body(): lax.all_gather(key_rows, 'ctx', axis=0, tiled=True)]
    all_to_all x4 -> x0, waiting for transfers between devices: 98.1 us -> none  [the longest x1 56.6 us: body(): lax.all_to_all(result[arrived_slot], 'ctx', split_axis=0, concat_axis=0,...]
    all_gather x2 -> x0, blocking collectives: 67.1 us -> none  [the longest x1 33.9 us: body(): lax.all_gather(log_total, 'ctx', axis=0, tiled=True)]
    dynamic_slice x27 -> x1, local copies, waits for them, and re-layouts: 65.4 us -> 0.59 us  [fast_body(): lax.dynamic_slice_in_dim(grad_scale, f * 20, 20)]
  transfers between devices with their start and end apart: 17 -> 0, of which waited for: 14 -> 0; matrix products, arithmetic and copies ran while one was open for 28% -> 0% of each run, Pallas kernels for 0% -> 0%
where the time goes in v2:
time: 350 us; the launch traced here: 347 us
  Pallas kernels  328 us (94%)
  other arithmetic  10.5 us (3%)
  local copies, waits for them, and re-layouts  7.44 us (2%)
    pallas_call x1, Pallas kernels, backward(): pl.pallas_call(backward_kernel, name='backward', out_shape=(shape((320, 1...  220 us
    pallas_call x1, Pallas kernels, forward(): pl.pallas_call(attend_kernel, name='forward', out_shape=(shape((1280, 256...  108 us

profile of v2, /device:TPU:0, one launch (start us, length us, event | category | flops | bytes accessed | tf_op | source)
XLA Modules:
  0.0 346.9 jit_solution(9922034042024612226)
XLA Ops:
  0.6 0.7 pad.15
  1.3 0.7 pad.16
  2.0 0.7 pad.17
  2.7 1.2 stack.23.aux_ref
  3.9 108.2 %forward.1 = (bf16[1280,256]{1,0:T(8,128)(2,1)}, bf16[2048,1280]{1,0:T(8,128)(2,1)}, bf16[2048,768]{1,0:T(8,128)(2,1)}, f32[8,2048]{1,0:T(8,128)}, bf16[160,2048...) custom-call(s32[1,4]{1,0:T(1,128)} %ends_ref.1, ...), custom_call_target="tpu_custom_call" | custom-call | flops 20000000000 | bytes 40000000 | tf_op jit(solution)/shard_map/forward/pallas_call | solution.py:805
  112.2 0.7 broadcast_multiply_fusion
  112.9 0.7 broadcast_in_dim.13.mult_ref
  113.6 0.0 copy-start
  113.6 220.0 %backward.1 = (bf16[320,1280]{1,0:T(8,128)(2,1)}, bf16[320,1280]{1,0:T(8,128)(2,1)}, bf16[320,1280]{1,0:T(8,128)(2,1)}, bf16[320,3840]{1,0:T(8,128)(2,1)}, f32[256,1280]{1,0:T(8,128)}, /*index=5*/f32[8,128]{1,0:T(8,128)}) custom-call(bf16[1280,256]{1,0:T(8,128)(2,1)} %get-tuple-element.31.grad_ref, bf16[1280,256]{1,0:T(8,128)(2,1)} %get-tuple-element.32.att_ref, ...), custom_call_target="tpu_custom_call" | custom-call | flops 30000001024 | bytes 60000000 | tf_op jit(solution)/shard_map/backward/pallas_call | solution.py:1378
  333.6 0.0 copy-done
  333.6 0.0 copy-start.6
  333.6 4.6 %multiply_reduce_fusion = (f32[320]{0:T(512)S(1)}, f32[320,3840]{1,0:T(8,128)}) fusion(bf16[320,3840]{1,0:T(8,128)(2,1)S(1)} %copy-done, bf16[320,3840]{1,0:T(8,128)(2,1)} %get-tuple-element.46), kind=kLoop, calls=%fused_computation | loop fusion | flops 4914880 | bytes 9831680 | tf_op jit(solution)/shard_map/reduce_sum | solution.py:1486
  338.3 0.0 copy-start.3
  338.3 0.0 copy-start.5
  338.3 0.0 copy-done.6
  338.3 1.3 convert_element_type.32
  339.5 0.0 copy-start.4
  339.5 0.1 copy-done.3
  339.7 0.6 copy-done.5
  340.2 1.4 multiply_reduce_fusion.1
  341.6 0.0 copy-done.4
  341.6 0.0 copy-start.2
  341.6 1.3 convert_element_type.34
  342.9 0.0 copy-done.7
  342.9 0.0 copy-done.8
  342.9 0.6 convert_divide_fusion
  343.5 0.7 divide_multiply_fusion
  344.2 0.6 dynamic_slice.3
  344.8 0.0 copy-done.1
  344.8 1.1 copy.22
  345.9 0.0 copy-done.2
  345.9 1.1 copy.23
  (10 shorter events, 0.0 us)
Async XLA Ops:
  113.6 220.0 %copy-start = (bf16[320,3840]{1,0:T(8,128)(2,1)S(1)}, bf16[320,3840]{1,0:T(8,128)(2,1)}, u32[]{:S(2)}) copy-start(bf16[320,3840]{1,0:T(8,128)(2,1)} %w_ref.1) | copy-start | bytes 7372804
  333.6 4.7 %copy-start.6 = (bf16[320,1280]{1,0:T(8,128)(2,1)S(1)}, bf16[320,1280]{1,0:T(8,128)(2,1)}, u32[]{:S(2)}) copy-start(bf16[320,1280]{1,0:T(8,128)(2,1)} %get-tuple-element.47) | copy-start | bytes 2457604
  338.3 1.4 copy-start.3
  338.3 2.0 copy-start.5
  339.5 2.1 copy-start.4
  341.6 1.3 copy-start.7
  341.6 1.3 copy-start.8
  341.6 3.2 copy-start.1
  341.6 4.2 %copy-start.2 = (f32[256,1280]{1,0:T(8,128)S(1)}, f32[256,1280]{1,0:T(8,128)}, u32[]{:S(2)}) copy-start(f32[256,1280]{1,0:T(8,128)} %get-tuple-element.45) | copy-start | bytes 3932164
